TPU v7x, 32 devices: a whole 2x2x4 slice. The times are simulated.
32 devices in a mesh: story: 8 (over y, x, core), col: 4 (over z).
Axes of the slice: x: 2, y: 2, z: 4, core: 2. Of those that a mesh axis runs over, the one named last changes fastest.
Arguments:
- inv_factor: bfloat16 [8, 2048, 2048], P('story', 'col'), may hold values from -1 to 1.5, as said below
- coupling_above: bfloat16 [8, 2048, 2048], P('story', 'col'), may hold values from -0.0029296875 to 0.0029296875
- coupling_below: bfloat16 [8, 2048, 2048], P('story', 'col'), may hold values from -0.0029296875 to 0.0029296875
- interior_loads: bfloat16 [8, 64, 2048], P('story'), may hold values from -18 to 18
- separator_loads: float32 [8, 64, 2048], P('story', None, 'col'), may hold values from -6 to 6
- lateral_pattern: bfloat16 [8, 2048], P('story'), may hold values from -0.03125 to 0.03125
- drift_pairs: int32 [256, 2], replicated, may hold values from 0 to 8, as said below
Outputs:
- solved_interior: float32 [8, 64, 2048], P('story', None, 'col')
- reduced_loads: float32 [8, 64, 2048], P('story', None, 'col')
- separator_update: float32 [8, 2048, 2048], P('story', 'col')
- separator_coupling: float32 [8, 2048, 2048], P('story', 'col')
- drift: float32 [256, 64], replicated
Inputs may be any that keep to these rules, and one draw needn't show every extreme that they name: `inv_factor`: each matrix is lower triangular with a positive diagonal. `drift_pairs`: every row has a_p < b_p; row 0 is (0, 8).
All inputs are finite; a program needn't handle non-finite values.
Results may differ from a plain program's by a relative error of at most 0.0035.
Values may be sent and summed in bfloat16 or wider, within the bound.
A program may use at most 128 MiB of HBM per device.

v0:
```python
import jax
import jax.numpy as jnp
from jax import lax
from jax.sharding import PartitionSpec as P


def from_behind(value, axis, steps):
    count = lax.axis_size(axis)
    first, last = (max(0, -steps), min(count, count - steps))
    return lax.ppermute(value, axis, [(source, source + steps) for source in range(first, last)])


def entering(shard, axis, combine, identity):
    devices, mine = (lax.axis_size(axis), lax.axis_index(axis))
    everything = lax.all_gather(shard, axis)
    start = jnp.broadcast_to(jnp.asarray(identity, shard.dtype), shard.shape)

    def lap(k, before):
        reached = k < mine
        new = combine(before, everything[k])
        return jnp.where(reached, new, before)

    return lax.fori_loop(0, devices, lap, start)


def transposed(first_operand, second_operand):
    return lax.dot_general(
        first_operand, second_operand, (((1,), (1,)), ((), ())), preferred_element_type=jnp.float32
    )


def add_terms(earlier, later):
    return earlier + later


def per_device(
    inv_factor,
    coupling_above,
    coupling_below,
    interior_loads,
    separator_loads,
    lateral_pattern,
    drift_pairs,
):
    inverse_rows = inv_factor[0]
    above_rows = coupling_above[0]
    below_rows = coupling_below[0]
    case_loads = interior_loads[0]
    sep_loads = separator_loads[0]
    pattern_full = lateral_pattern[0]
    row_share = inverse_rows.shape[0]
    case_count = case_loads.shape[0]
    offset = lax.axis_index("col") * row_share
    operands = jnp.concatenate([above_rows, below_rows, case_loads], 0)
    panel_rows = transposed(operands, lax.all_gather(inverse_rows, "col", axis=0, tiled=True))
    factor_above = panel_rows[:row_share].astype(jnp.bfloat16)
    factor_below = panel_rows[row_share : 2 * row_share].astype(jnp.bfloat16)
    solved_full = panel_rows[2 * row_share :]
    solved_rows = lax.dynamic_slice_in_dim(solved_full, offset, row_share, 1)
    solved_half = solved_full.astype(jnp.bfloat16)
    pattern_rows = jnp.dot(inverse_rows, pattern_full, preferred_element_type=jnp.float32)
    story_part = jnp.dot(solved_rows, pattern_rows, precision=lax.Precision.HIGHEST)
    next_rows, next_solved = from_behind((factor_below, solved_half), "story", -1)
    stacked = jnp.stack([factor_above, factor_below, next_rows])
    gathered = lax.all_gather(stacked, "col", axis=1, tiled=True)
    products = jnp.stack(
        [
            transposed(factor_above, gathered[0]),
            transposed(factor_above, gathered[1]),
            transposed(next_rows, gathered[2]),
        ]
    )
    update = products[0] + products[2]
    coupling = -products[1]
    reduced = sep_loads - transposed(solved_half, factor_above) - transposed(next_solved, next_rows)
    stories = lax.axis_size("story")
    columns = lax.axis_size("col")
    first_story = drift_pairs[:, 0]
    end_story = drift_pairs[:, 1]
    running = entering(story_part, "story", add_terms, jnp.zeros_like(story_part))
    running_all, part_all = (
        lax.all_gather(running[None], ("story", "col"), axis=0, tiled=True),
        lax.all_gather(story_part[None], ("story", "col"), axis=0, tiled=True),
    )
    running_sum = running_all.reshape(stories, columns, case_count).sum(1)
    part_sum = part_all.reshape(stories, columns, case_count).sum(1)
    extended = jnp.concatenate([running_sum, running_sum[-1:] + part_sum[-1:]], 0)
    levels = jnp.arange(stories + 1, dtype=jnp.int32)
    weights = (levels[None, :] == end_story[:, None]).astype(jnp.float32) - (
        levels[None, :] == first_story[:, None]
    ).astype(jnp.float32)
    drift = jnp.dot(weights, extended, precision=lax.Precision.HIGHEST)
    return (solved_rows[None], reduced[None], update[None], coupling[None], drift)


def solution(mesh):
    placed = (
        P("story", "col", None),
        P("story", "col", None),
        P("story", "col", None),
        P("story", None, None),
        P("story", None, "col"),
        P("story", None),
        P(),
    )
    return jax.shard_map(
        per_device,
        mesh=mesh,
        in_specs=placed,
        out_specs=(
            P("story", None, "col"),
            P("story", None, "col"),
            P("story", "col", None),
            P("story", "col", None),
            P(),
        ),
        check_vma=False,
    )
```

profile of v0, /device:TPU:13, one launch (start us, length us, event | category | flops | bytes accessed | tf_op | source)
XLA Modules:
  0.0 666.1 jit_solution(7755745467541471742)
XLA Ops:
  7.2 0.0 copy-start
  7.2 0.0 all-gather.9.cloned.1.call-start
  7.2 0.7 all-gather.9.cloned.1.call-update
  7.9 0.0 all-gather.7.cloned.1.call-start
  8.0 149.7 %all-gather.9.cloned.1.call-done = bf16[1,2048,2048]{2,1,0:T(8,128)(2,1)} async-done(((bf16[1,512,2048]{2,1,0:T(8,128)(2,1)}), bf16[1,2048,2048]{2,1,0:T(8,128)(2,1)}) %all-gather.9.cloned.1.call-update) | async-done | bytes 8388624 | tf_op jit(solution)/shard_map/all_gather | solution.py:55
  157.6 15.4 %fusion.38 = (bf16[1088,2048]{1,0:T(8,128)(2,1)S(1)}, f32[1088,2048]{1,0:T(8,128)}) fusion(bf16[1,2048,2048]{2,1,0:T(8,128)(2,1)} %all-gather.9.cloned.1.call-done, bf16[64,2048]{1,0:T(8,128)(2,1)} %bitcast.65, bf16[512,2048]{1,0:T(8,128)(2,1)} %bitcast.63, bf16[512,2048]{1,0:T(8,128)(2,1)} %bitcast.64), kind=kOutput, calls=%fused_computation.51 | convolution fusion | flops 9142403072 | bytes 26214400 | tf_op jit(solution)/shard_map/dot_general | solution.py:27
  173.0 0.0 copy-start.2
  173.0 0.8 slice_bitcast_fusion.10
  173.8 1.3 copy-done.2
  175.1 2.6 collective-permute-start.1
  177.7 24.8 %collective-permute-done.1 = bf16[512,2048]{1,0:T(8,128)(2,1)S(1)} collective-permute-done((bf16[512,2048]{1,0:T(8,128)(2,1)S(1)}, bf16[512,2048]{1,0:T(8,128)(2,1)S(1)}, u32[]{:S(2)}, u32[]{:S(2)}) %collective-permute-start.1) | collective-permute-done | bytes 2097184 | tf_op jit(solution)/shard_map/ppermute | solution.py:10
  202.5 0.0 copy-start.4
  202.5 1.3 copy-done.4
  203.8 3.2 pad_maximum_fusion
  207.0 0.0 copy-start.8
  207.0 0.0 copy-start.3
  207.0 0.0 all-gather.7.cloned.1.call-update
  207.0 0.6 copy-done.8
  207.6 0.6 dynamic-slice
  208.9 0.0 copy-done.7
  208.9 0.0 copy-done
  208.9 0.0 copy-done.3
  208.9 0.6 fusion.20
  209.5 1.2 slice.71
  210.8 1.1 slice.42
  211.9 0.2 convolution_bitcast_fusion
  212.1 0.2 dynamic-update-slice
  212.3 11.0 %all-reduce = f32[512]{0:T(512)S(1)} all-reduce(f32[512]{0:T(512)S(1)} %dynamic-update-slice), channel_id=3, replica_groups=mesh['story'=8,'col'=4] {'story'}, use_global_device_ids=true, to_apply=%add | all-reduce | flops 512 | bytes 4096
  223.2 0.1 reshape.19
  223.3 0.2 dynamic-update-slice.2
  223.5 0.3 while.14
  223.8 0.3 dynamic-update-slice.1
  224.1 65.6 %all-reduce.3 = (f32[2048]{0:T(1024)S(1)}, f32[2048]{0:T(1024)S(1)}) all-reduce(f32[2048]{0:T(1024)S(1)} %dynamic-update-slice.2, f32[2048]{0:T(1024)S(1)} %dynamic-update-slice.1), channel_id=5, replica_groups=mesh['story'=8,'col'=4] {'story','col'}, use_global_device_ids=true, to_apply=%add.2 | all-reduce | flops 4096 | bytes 32768
  289.7 0.1 reshape.17
  289.7 0.1 reshape.16
  289.8 4.5 collective-permute-start
  294.3 0.7 dynamic-slice_bitcast_fusion
  295.0 1.0 fusion.23
  296.0 0.0 copy-done.6
  296.0 2.5 fusion.16
  298.6 0.2 collective-permute-done
  298.8 0.0 copy-done.5
  298.8 1.4 fusion.19
  300.2 331.0 %all-gather.7.cloned.1.call-done = bf16[3,2048,2048]{2,1,0:T(8,128)(2,1)} async-done(((bf16[3,512,2048]{2,1,0:T(8,128)(2,1)}), bf16[3,2048,2048]{2,1,0:T(8,128)(2,1)}) %all-gather.7.cloned.1.call-update) | async-done | bytes 25165840 | tf_op jit(solution)/shard_map/all_gather | solution.py:65
  631.2 7.0 %fusion.1 = f32[512,2048]{1,0:T(8,128)S(1)} fusion(bf16[512,2048]{1,0:T(8,128)(2,1)S(1)} %copy-done.5, bf16[3,2048,2048]{2,1,0:T(8,128)(2,1)} %all-gather.7.cloned.1.call-done), kind=kOutput, calls=%fused_computation.5 | convolution fusion | flops 4294967296 | bytes 14680064 | tf_op jit(solution)/shard_map/dot_general | solution.py:27
  638.2 10.6 %negate_bitcast_fusion = f32[1,512,2048]{2,1,0:T(8,128)} fusion(bf16[3,2048,2048]{2,1,0:T(8,128)(2,1)} %all-gather.7.cloned.1.call-done, bf16[1088,2048]{1,0:T(8,128)(2,1)} %copy-done.2), kind=kOutput, calls=%fused_computation.16 | convolution fusion | flops 4296015872 | bytes 14680064 | tf_op jit(solution)/shard_map/dot_general | solution.py:27
  648.7 10.6 %add_bitcast_fusion = f32[1,512,2048]{2,1,0:T(8,128)} fusion(f32[512,2048]{1,0:T(8,128)S(1)} %fusion.1, bf16[3,2048,2048]{2,1,0:T(8,128)(2,1)} %all-gather.7.cloned.1.call-done, bf16[1088,2048]{1,0:T(8,128)(2,1)} %copy-done.2), kind=kOutput, calls=%fused_computation.17 | convolution fusion | flops 4296015872 | bytes 18874368 | tf_op jit(solution)/shard_map/dot_general | solution.py:27
  659.3 0.0 copy-done.1
  (20 shorter events, 0.2 us)
Async XLA Ops:
  7.2 201.7 %copy-start = (bf16[1,2048]{1,0:T(2,128)(2,1)S(1)}, bf16[1,2048]{1,0:T(2,128)(2,1)}, u32[]{:S(2)}) copy-start(bf16[1,2048]{1,0:T(2,128)(2,1)} %param.14) | copy-start | bytes 12292
  7.2 150.4 %all-gather.9.cloned.1.call-start = ((), (), s32[]{:S(2)}) async-start(), calls=%async_computation.1 | async-start | bytes 10485760 | tf_op jit(solution)/shard_map/all_gather | solution.py:55
  7.9 623.3 %all-gather.7.cloned.1.call-start = ((), (), s32[]{:S(2)}) async-start(), calls=%async_computation | async-start | bytes 31457280 | tf_op jit(solution)/shard_map/all_gather | solution.py:65
  173.0 2.1 copy-start.2
  175.1 27.4 %collective-permute-start.1 = (bf16[512,2048]{1,0:T(8,128)(2,1)S(1)}, bf16[512,2048]{1,0:T(8,128)(2,1)S(1)}, u32[]{:S(2)}, u32[]{:S(2)}) collective-permute-start(bf16[512,2048]{1,0:T(8,128)(2,1)S(1)} %get-tuple-element.112), channel_id=1, source_target_pairs={{4,0},{8,4},{12,8},{16,12},{20,16},{24,20},{28,24},{5,1},{9,5},{13... | collective-permute-start | bytes 6291464 | tf_op jit(solution)/shard_map/ppermute | solution.py:10
  202.5 1.3 copy-start.4
  207.0 0.7 copy-start.8
  207.0 1.9 copy-start.7
  207.0 1.9 copy-start.3
  207.0 89.1 %copy-start.6 = (f32[1,64,512]{2,1,0:T(8,128)S(1)}, f32[1,64,512]{2,1,0:T(8,128)}, u32[]{:S(2)}) copy-start(f32[1,64,512]{2,1,0:T(8,128)} %param.13) | copy-start | bytes 393220
  209.5 89.2 %copy-start.5 = (bf16[512,2048]{1,0:T(8,128)(2,1)S(1)}, bf16[512,2048]{1,0:T(8,128)(2,1)}, u32[]{:S(2)}) copy-start(bf16[512,2048]{1,0:T(8,128)(2,1)} %copy-done.4) | copy-start | bytes 6291460
  289.8 8.9 %collective-permute-start = (bf16[64,2048]{1,0:T(8,128)(2,1)S(1)}, bf16[64,2048]{1,0:T(8,128)(2,1)S(1)}, u32[]{:S(2)}, u32[]{:S(2)}) collective-permute-start(bf16[64,2048]{1,0:T(8,128)(2,1)S(1)} %slice.71), channel_id=1, source_target_pairs={{4,0},{8,4},{12,8},{16,12},{20,16},{24,20},{28,24},{5,1},{9,5},{13... | collective-permute-start | bytes 786440 | tf_op jit(solution)/shard_map/ppermute | solution.py:10
  648.7 10.6 %copy-start.1 = (bf16[1,2048]{1,0:T(2,128)(2,1)S(1)}, bf16[1,2048]{1,0:T(2,128)(2,1)}, u32[]{:S(2)}) copy-start(bf16[1,2048]{1,0:T(2,128)(2,1)} %param.14) | copy-start | bytes 12292
Sparse Core Ops, SparseCore 0:
  9.6 147.9 all-gather.8
  207.1 424.0 all-gather.6
where the time goes:
time: 671 us; the launch traced here: 666 us
  waiting for transfers between devices  506 us (75%)
  blocking collectives  76.6 us (11%)
  matrix products  49.3 us (7%)
  between operations  14.9 us (2%)
  local copies, waits for them, and re-layouts  8.47 us (1%)
  starting transfers between devices  7.12 us (1%)
    all_gather x1, waiting for transfers between devices, per_device(): gathered = lax.all_gather(stacked, 'col', axis=1, tiled=True)  331 us
    all_gather x1, waiting for transfers between devices, per_device(): lax.all_gather(inverse_rows, 'col', axis=0, tiled=True)  150 us
    unnamed x2, blocking collectives  76.6 us
    dot_general x6, matrix products, transposed(): lax.dot_general(first_operand, second_operand, (((1,), (1,)), ((), ())),...  47.5 us
    ppermute x2, waiting for transfers between devices, from_behind(): lax.ppermute(value, axis, [(source, source + steps) for source in range(f...  24.9 us
  transfers between devices with their start and end apart: 4, of which 4 were waited for; matrix products, arithmetic and copies ran while one was open for 2% of the time, Pallas kernels for 0%

commit v1 on v0

v1 whole, which is shorter than its diff:
```python
import jax
import jax.numpy as jnp
from jax import lax
from jax.sharding import PartitionSpec as P

BF16 = jnp.bfloat16
F32 = jnp.float32


def across(value, axis, pairs):
    return lax.ppermute(value, axis, pairs)


def from_above(value):
    count = lax.axis_size("story")
    return lax.ppermute(value, "story", [(j + 1, j) for j in range(count - 1)])


def transposed(first_operand, second_operand):
    return lax.dot_general(first_operand, second_operand, (((1,), (1,)), ((), ())), preferred_element_type=F32)


def drift_of(story_part, drift_pairs):
    stories = lax.axis_size("story")
    levels = jnp.arange(stories, dtype=jnp.int32)
    mine = (levels == lax.axis_index("story"))[:, None]
    work = lax.psum(jnp.where(mine, story_part[None, :], 0.0), ("story", "col"))
    first_story = drift_pairs[:, 0]
    end_story = drift_pairs[:, 1]
    inside = (levels[None, :] >= first_story[:, None]) & (levels[None, :] < end_story[:, None])
    return jnp.dot(inside.astype(F32), work, precision=lax.Precision.HIGHEST)


def gathered_form(inverse, above, below, loads, sep_loads):
    share = inverse.shape[0]
    operands = jnp.concatenate([above, below, loads], 0)
    panel = transposed(operands, lax.all_gather(inverse, "col", axis=0, tiled=True))
    factors = panel[: 2 * share].astype(BF16)
    factor_above, factor_below = factors[:share], factors[share:]
    solved_half = panel[2 * share :].astype(BF16)
    whole = lax.all_gather(jnp.stack([factor_above, factor_below]), "col", axis=1, tiled=True)
    square_below = transposed(factor_below, whole[1]).astype(BF16)
    loads_below = transposed(solved_half, factor_below)
    next_square, next_loads = from_above((square_below, loads_below))
    update = transposed(factor_above, whole[0]) + next_square.astype(F32)
    coupling = -transposed(factor_above, whole[1])
    reduced = sep_loads - transposed(solved_half, factor_above) - next_loads
    return reduced, update, coupling


def middle_form(inverse, above, below, loads, sep_loads):
    share = inverse.shape[0]
    half = share // 2
    width = 4 * share
    col = lax.axis_index("col")
    right = col == 2

    def widened(value):
        return jnp.pad(value, ((0, 0), (0, width - value.shape[1])))

    inv_1to2 = across(inverse[:, : 2 * share], "col", [(1, 2)])
    inv_0to1 = across(inverse[:, :share], "col", [(0, 1)])
    inv_0to2 = across(inverse[:, :share], "col", [(0, 2)])
    inv_3to2 = across(inverse, "col", [(3, 2)])
    inv_2to1 = across(inverse[:, : 3 * share], "col", [(2, 1)])
    inv_3to1 = across(inv_3to2, "col", [(2, 1)])

    def chunk(part):
        rows = slice(part * half, (part + 1) * half)
        return jnp.concatenate([above[rows], below[rows]], 0)

    own_c = [chunk(0), chunk(1)]
    end_c = [across(piece, "col", [(0, 1), (3, 2)]) for piece in own_c]
    om_c = [across(piece, "col", [(1, 2)]) for piece in own_c]
    oe_c = []
    for piece, before in zip(end_c, om_c):
        piece, _ = lax.optimization_barrier((piece, before))
        oe_c.append(across(piece, "col", [(1, 2)]))

    inv_end = widened(inv_0to1) + inv_3to2
    inv_om = widened(inv_1to2) + widened(inv_2to1)
    inv_oe = widened(inv_0to2) + inv_3to1
    inv_all = jnp.concatenate([inverse, inv_end, inv_om, inv_oe], 0)

    solved_half = transposed(loads, inv_all).astype(BF16)
    solved_two = jnp.concatenate([solved_half, from_above(solved_half)], 1)

    def factored(pieces):
        product = [transposed(piece, inv_all).astype(BF16) for piece in pieces]
        a = jnp.concatenate([piece[:half] for piece in product], 0)
        b = jnp.concatenate([piece[half:] for piece in product], 0)
        return a, b, jnp.concatenate([a, from_above(b)], 1)

    a_own, b_own, w_own = factored(own_c)
    a_end, b_end, w_end = factored(end_c)
    b_near = jnp.concatenate([b_own, b_end], 0)
    w_near = jnp.concatenate([w_own, w_end], 0)

    up_own_near = transposed(w_own, w_near)
    cp_own_near = -transposed(a_own, b_near)
    up_end_near = transposed(w_end, w_near).astype(BF16)
    cp_end_near = (-transposed(a_end, b_near)).astype(BF16)
    near_pair = across(jnp.stack([up_end_near, cp_end_near]), "col", [(1, 0), (2, 3)])
    taken_own = transposed(solved_two, w_own)
    taken_end = across(transposed(solved_two, w_end), "col", [(1, 0), (2, 3)])

    a_om, b_om, w_om = factored(om_c)
    om_back = across(
        jnp.stack([transposed(w_om, w_near).astype(BF16), (-transposed(a_om, b_near)).astype(BF16)]), "col", [(2, 1)]
    )
    om_out = across(
        jnp.stack([transposed(w_end, w_om).astype(BF16), (-transposed(a_end, b_om)).astype(BF16)]), "col", [(2, 3)]
    )
    up_own_om, cp_own_om = transposed(w_own, w_om), -transposed(a_own, b_om)

    oe_back, oe_out, up_own_oe, cp_own_oe = [], [], [], []
    for piece in oe_c:
        a_oe, b_oe, w_oe = factored([piece])
        oe_back.append(
            across(
                jnp.stack([transposed(w_oe, w_near).astype(BF16), (-transposed(a_oe, b_near)).astype(BF16)]),
                "col",
                [(2, 0)],
            )
        )
        oe_out.append(
            across(
                jnp.stack([transposed(w_end, w_oe).astype(BF16), (-transposed(a_end, b_oe)).astype(BF16)]),
                "col",
                [(2, 3)],
            )
        )
        up_own_oe.append(transposed(w_own, w_oe))
        cp_own_oe.append(-transposed(a_own, b_oe))
    oe_back = jnp.concatenate(oe_back, 1)

    def assembled(which, own_near, own_om, own_oe):
        near = near_pair[which].astype(F32)
        swap = lambda pair: jnp.concatenate([pair[:, share:], pair[:, :share]], 1)
        row_0 = jnp.concatenate([swap(near), oe_back[which].astype(F32)], 1)
        row_1 = jnp.concatenate([swap(own_near), om_back[which].astype(F32)], 1)
        row_2 = jnp.concatenate([*own_oe, own_om, own_near], 1)
        row_3 = jnp.concatenate(
            [*[piece[which].astype(F32) for piece in oe_out], om_out[which].astype(F32), near], 1
        )
        low = jnp.where(col == 0, row_0, row_1)
        high = jnp.where(right, row_2, row_3)
        return jnp.where(col < 2, low, high)

    update = assembled(0, up_own_near, up_own_om, up_own_oe)
    coupling = assembled(1, cp_own_near, cp_own_om, cp_own_oe)
    middle = (col == 1) | right
    reduced = sep_loads - jnp.where(middle, taken_own, taken_end)
    return reduced, update, coupling


def per_device(
    inv_factor,
    coupling_above,
    coupling_below,
    interior_loads,
    separator_loads,
    lateral_pattern,
    drift_pairs,
):
    inverse = inv_factor[0]
    loads = interior_loads[0]
    solved_rows = transposed(loads, inverse)
    pattern_rows = jnp.dot(inverse, lateral_pattern[0], preferred_element_type=F32)
    story_part = jnp.dot(solved_rows, pattern_rows, precision=lax.Precision.HIGHEST)
    form = middle_form if lax.axis_size("col") == 4 else gathered_form
    reduced, update, coupling = form(inverse, coupling_above[0], coupling_below[0], loads, separator_loads[0])
    drift = drift_of(story_part, drift_pairs)
    return (solved_rows[None], reduced[None], update[None], coupling[None], drift)


def solution(mesh):
    placed = (
        P("story", "col", None),
        P("story", "col", None),
        P("story", "col", None),
        P("story", None, None),
        P("story", None, "col"),
        P("story", None),
        P(),
    )
    return jax.shard_map(
        per_device,
        mesh=mesh,
        in_specs=placed,
        out_specs=(
            P("story", None, "col"),
            P("story", None, "col"),
            P("story", "col", None),
            P("story", "col", None),
            P(),
        ),
        check_vma=False,
    )
```

time: 671 us -> 587 us (0.87)
  waiting for transfers between devices: 506 us -> 130 us
  matrix products: 49.3 us -> 178 us
  other arithmetic: 3.35 us -> 82.9 us
  starting transfers between devices: 7.12 us -> 61.1 us
  blocking collectives: 76.6 us -> 99.1 us
  local copies, waits for them, and re-layouts: 8.47 us -> 27.8 us
  between operations: 14.9 us -> 1.98 us
    all_gather x2 -> x0, waiting for transfers between devices: 481 us -> none  [the longest x1 331 us: per_device(): gathered = lax.all_gather(stacked, 'col', axis=1, tiled=True)]
    dot_general x6 -> x34, matrix products: 47.5 us -> 177 us  [transposed(): lax.dot_general(first_operand, second_operand, (((1,), (1,)), ((), ())),...]
    ppermute x2 -> x26, waiting for transfers between devices: 24.9 us -> 130 us  [the longest x20 89.8 us: across(): return lax.ppermute(value, axis, pairs)]
    psum x0 -> x1, blocking collectives: none -> 99.1 us  [drift_of(): work = lax.psum(jnp.where(mine, story_part[None, :], 0.0), ('story', 'col'))]
    unnamed x2 -> x0, blocking collectives: 76.6 us -> none
    concatenate x0 -> x6, other arithmetic: none -> 55.3 us  [the longest x1 47.3 us: middle_form(): w_near = jnp.concatenate([w_own, w_end], 0)]
    ppermute x2 -> x26, starting transfers between devices: 7.05 us -> 61.1 us  [the longest x20 44.7 us: across(): return lax.ppermute(value, axis, pairs)]
    slice x3 -> x16, local copies, waits for them, and re-layouts: 2.32 us -> 17 us  [the longest x6 5.99 us: factored(): a = jnp.concatenate([piece[:half] for piece in product], 0)]
  transfers between devices with their start and end apart: 4 -> 26, of which waited for: 4 -> 6; matrix products, arithmetic and copies ran while one was open for 2% -> 44% of each run, Pallas kernels for 0% -> 0%
where the time goes in v1:
time: 587 us; the launch traced here: 581 us
  matrix products  178 us (30%)
  waiting for transfers between devices  130 us (22%)
  blocking collectives  99.1 us (17%)
  other arithmetic  82.9 us (14%)
  starting transfers between devices  61.1 us (10%)
  local copies, waits for them, and re-layouts  27.8 us (5%)
    dot_general x34, matrix products, transposed(): lax.dot_general(first_operand, second_operand, (((1,), (1,)), ((), ())),...  177 us
    psum x1, blocking collectives, drift_of(): work = lax.psum(jnp.where(mine, story_part[None, :], 0.0), ('story', 'col'))  99.1 us
    ppermute x20, waiting for transfers between devices, across(): return lax.ppermute(value, axis, pairs)  89.8 us
    concatenate x1, other arithmetic, middle_form(): w_near = jnp.concatenate([w_own, w_end], 0)  47.3 us
    ppermute x20, starting transfers between devices, across(): return lax.ppermute(value, axis, pairs)  44.7 us
    ppermute x6, waiting for transfers between devices, from_above(): return lax.ppermute(value, 'story', [(j + 1, j) for j in range(count - 1)])  40.4 us
    ppermute x6, starting transfers between devices, from_above(): return lax.ppermute(value, 'story', [(j + 1, j) for j in range(count - 1)])  16.4 us
  transfers between devices with their start and end apart: 26, of which 6 were waited for; matrix products, arithmetic and copies ran while one was open for 44% of the time, Pallas kernels for 0%

profile of v1, /device:TPU:13, one launch (start us, length us, event | category | flops | bytes accessed | tf_op | source)
XLA Modules:
  0.0 581.4 jit_solution(18205187957749832381)
XLA Ops:
  4.1 2.7 collective-permute-start.2
  13.1 5.4 collective-permute-start.17
  20.2 8.4 %collective-permute-done.2 = bf16[512,1024]{1,0:T(8,128)(2,1)S(1)} collective-permute-done((bf16[512,1024]{1,0:T(8,128)(2,1)S(1)}, bf16[512,1024]{1,0:T(8,128)(2,1)S(1)}, u32[]{:S(2)}, u32[]{:S(2)}) %collective-permute-start.2) | collective-permute-done | bytes 1048608 | tf_op jit(solution)/shard_map/ppermute | solution.py:11
  29.8 15.4 %collective-permute-done.3 = bf16[512,1536]{1,0:T(8,128)(2,1)S(1)} collective-permute-done((bf16[512,1536]{1,0:T(8,128)(2,1)S(1)}, bf16[512,1536]{1,0:T(8,128)(2,1)S(1)}, u32[]{:S(2)}, u32[]{:S(2)}) %collective-permute-start.3) | collective-permute-done | bytes 1572896 | tf_op jit(solution)/shard_map/ppermute | solution.py:11
  46.4 2.7 collective-permute-start.13
  53.6 6.7 %collective-permute-done.9 = bf16[512,2048]{1,0:T(8,128)(2,1)} collective-permute-done((bf16[512,2048]{1,0:T(8,128)(2,1)}, bf16[512,2048]{1,0:T(8,128)(2,1)}, u32[]{:S(2)}, u32[]{:S(2)}) %collective-permute-start.9) | collective-permute-done | bytes 2097184 | tf_op jit(solution)/shard_map/ppermute | solution.py:11
  61.5 99.1 %psum.7 = f32[8,64]{1,0:T(8,128)S(1)} all-reduce(f32[8,64]{1,0:T(8,128)S(1)} %broadcast_select_fusion), channel_id=1, replica_groups=mesh['story'=8,'col'=4] {'story','col'}, use_global_device_ids=true, to_apply=%region_0.1 | all-reduce | flops 512 | bytes 4096 | tf_op jit(solution)/shard_map/psum | solution.py:27
  164.6 5.1 collective-permute-start.18
  169.7 2.8 collective-permute-start.14
  174.6 4.0 pad_add_fusion
  178.6 9.7 %convolution_convert_fusion.7 = bf16[512,2048]{1,0:T(8,128)(2,1)} fusion(bf16[256,2048]{1,0:T(8,128)(2,1)S(1)} %copy-done.16, bf16[256,2048]{1,0:T(8,128)(2,1)S(1)} %copy-done.18, bf16[512,2048]{1,0:T(8,128)(2,1)} %pad_add_fusion, bf16[512,2048]{1,0:T(8,128)(2,1)S(1)} %pad_add_fusion.1, bf16[512,2048]{1,0:T(8,128)(2,1)S(1)} %pad_add_fusion.2, ...), kind=kOutput, calls=%fused_computation.19 | convolution fusion | flops 4333764608 | bytes 12582912 | tf_op jit(solution)/shard_map/dot_general | solution.py:20
  188.4 9.8 %convolution_convert_fusion.6 = bf16[512,2048]{1,0:T(8,128)(2,1)} fusion(bf16[256,2048]{1,0:T(8,128)(2,1)S(1)} %get-tuple-element.44, bf16[256,2048]{1,0:T(8,128)(2,1)S(1)} %copy-done.14, bf16[512,2048]{1,0:T(8,128)(2,1)} %pad_add_fusion, bf16[512,2048]{1,0:T(8,128)(2,1)S(1)} %pad_add_fusion.1, bf16[512,2048]{1,0:T(8,128)(2,1)S(1)} %pad_add_fusion.2, ...), kind=kOutput, calls=%fused_computation.18 | convolution fusion | flops 4333764608 | bytes 12582912 | tf_op jit(solution)/shard_map/dot_general | solution.py:20
  200.3 13.4 %convolution_convert_fusion.4 = bf16[512,2048]{1,0:T(8,128)(2,1)} fusion(bf16[512,2048]{1,0:T(8,128)(2,1)} %collective-permute-done.9, bf16[512,2048]{1,0:T(8,128)(2,1)S(1)} %copy-done.27, bf16[512,2048]{1,0:T(8,128)(2,1)S(1)} %pad_add_fusion.1, bf16[512,2048]{1,0:T(8,128)(2,1)S(1)} %pad_add_fusion.2, bf16[512,2048]{1,0:T(8,128)(2,1)S(1)} %bitcast.119), kind=kOutput, calls=%fused_computation.16 | convolution fusion | flops 4329570304 | bytes 12582912 | tf_op jit(solution)/shard_map/dot_general | solution.py:20
  217.3 11.3 %convolution_convert_fusion.5 = bf16[512,2048]{1,0:T(8,128)(2,1)} fusion(bf16[512,2048]{1,0:T(8,128)(2,1)} %collective-permute-done.8, bf16[512,2048]{1,0:T(8,128)(2,1)} %pad_add_fusion, bf16[512,2048]{1,0:T(8,128)(2,1)S(1)} %pad_add_fusion.1, bf16[512,2048]{1,0:T(8,128)(2,1)S(1)} %copy-done.24, bf16[512,2048]{1,0:T(8,128)(2,1)S(1)} %bitcast.120), kind=kOutput, calls=%fused_computation.17 | convolution fusion | flops 4329570304 | bytes 12582912 | tf_op jit(solution)/shard_map/dot_general | solution.py:20
  230.5 11.7 %convolution_convert_fusion.2 = bf16[512,2048]{1,0:T(8,128)(2,1)} fusion(bf16[512,2048]{1,0:T(8,128)(2,1)} %collective-permute-done.18, bf16[512,2048]{1,0:T(8,128)(2,1)} %pad_add_fusion, bf16[512,2048]{1,0:T(8,128)(2,1)S(1)} %pad_add_fusion.1, bf16[512,2048]{1,0:T(8,128)(2,1)S(1)} %copy-done.24, bf16[512,2048]{1,0:T(8,128)(2,1)S(1)} %bitcast.121), kind=kOutput, calls=%fused_computation.14 | convolution fusion | flops 4329570304 | bytes 12582912 | tf_op jit(solution)/shard_map/dot_general | solution.py:20
  242.2 2.9 fusion.29
  247.3 3.4 fusion.11
  252.2 11.5 %convolution_convert_fusion = bf16[512,2048]{1,0:T(8,128)(2,1)} fusion(bf16[512,2048]{1,0:T(8,128)(2,1)} %collective-permute-done.17, bf16[512,2048]{1,0:T(8,128)(2,1)} %pad_add_fusion, bf16[512,2048]{1,0:T(8,128)(2,1)S(1)} %pad_add_fusion.1, bf16[512,2048]{1,0:T(8,128)(2,1)S(1)} %copy-done.24, bf16[512,2048]{1,0:T(8,128)(2,1)S(1)} %bitcast.122), kind=kOutput, calls=%fused_computation.12 | convolution fusion | flops 4329570304 | bytes 12582912 | tf_op jit(solution)/shard_map/dot_general | solution.py:20
  265.9 11.5 %convolution_convert_fusion.1 = bf16[512,2048]{1,0:T(8,128)(2,1)} fusion(bf16[512,2048]{1,0:T(8,128)(2,1)} %collective-permute-done.13, bf16[512,2048]{1,0:T(8,128)(2,1)} %pad_add_fusion, bf16[512,2048]{1,0:T(8,128)(2,1)S(1)} %copy-done.21, bf16[512,2048]{1,0:T(8,128)(2,1)} %copy-done.23, bf16[512,2048]{1,0:T(8,128)(2,1)S(1)} %bitcast.123), kind=kOutput, calls=%fused_computation.13 | convolution fusion | flops 4329570304 | bytes 12582912 | tf_op jit(solution)/shard_map/dot_general | solution.py:20
  277.5 2.8 fusion.64
  290.8 3.4 fusion.2
  294.2 10.5 %convolution_convert_fusion.3 = bf16[512,2048]{1,0:T(8,128)(2,1)} fusion(bf16[512,2048]{1,0:T(8,128)(2,1)} %collective-permute-done.14, bf16[512,2048]{1,0:T(8,128)(2,1)} %pad_add_fusion, bf16[512,2048]{1,0:T(8,128)(2,1)} %copy-done.20, bf16[512,2048]{1,0:T(8,128)(2,1)} %copy-done.23, bf16[512,2048]{1,0:T(8,128)(2,1)S(1)} %bitcast.125), kind=kOutput, calls=%fused_computation.15 | convolution fusion | flops 4329570304 | bytes 12582912 | tf_op jit(solution)/shard_map/dot_general | solution.py:20
  304.7 3.0 fusion.25
  308.0 4.6 collective-permute-start.6
  314.5 3.5 collective-permute-start.19
  324.5 3.4 fusion.12
  333.3 40.4 %collective-permute-done.10 = bf16[512,2048]{1,0:T(8,128)(2,1)S(1)} collective-permute-done((bf16[512,2048]{1,0:T(8,128)(2,1)S(1)}, bf16[512,2048]{1,0:T(8,128)(2,1)S(1)}, u32[]{:S(2)}, u32[]{:S(2)}) %collective-permute-start.10) | collective-permute-done | bytes 2097184 | tf_op jit(solution)/shard_map/ppermute | solution.py:16
  373.7 3.2 fusion.35
  376.8 4.5 collective-permute-start.11
  381.4 2.6 fusion.32
  386.3 2.5 fusion.31
  391.2 47.3 %maximum_maximum_fusion = bf16[1024,4096]{1,0:T(8,128)(2,1)S(1)} fusion(bf16[512,2048]{1,0:T(8,128)(2,1)S(1)} %collective-permute-done.10, bf16[256,2048]{1,0:T(8,128)(2,1)S(1)} %get-tuple-element.39, bf16[256,2048]{1,0:T(8,128)(2,1)} %copy-done.8, bf16[512,2048]{1,0:T(8,128)(2,1)S(1)} %collective-permute-done.7, bf16[256,2048]{1,0:T(8,128)(2,1)S(1)} %get-tuple-element.35, ...), kind=kLoop, calls=%fused_computation.1 | loop fusion | flops 50331648 | bytes 16777216 | tf_op jit(solution)/shard_map/concatenate | solution.py:97
  438.6 3.7 fusion.19
  445.0 7.1 %fusion.9 = bf16[1,512,1024]{2,1,0:T(8,128)(2,1)} fusion(bf16[1024,4096]{1,0:T(8,128)(2,1)S(1)} %maximum_maximum_fusion, bf16[512,2048]{1,0:T(8,128)(2,1)} %copy-done.39, bf16[256,2048]{1,0:T(8,128)(2,1)S(1)} %get-tuple-element.39, bf16[256,2048]{1,0:T(8,128)(2,1)S(1)} %copy-done.9), kind=kOutput, calls=%fused_computation.45 | convolution fusion | flops 4308074496 | bytes 13631488 | tf_op jit(solution)/shard_map/dot_general | solution.py:20
  452.1 3.2 pad_maximum_fusion.11
  455.3 6.1 %fusion.62 = f32[512,1024]{1,0:T(8,128)S(1)} fusion(bf16[1024,4096]{1,0:T(8,128)(2,1)S(1)} %maximum_maximum_fusion, bf16[512,2048]{1,0:T(8,128)(2,1)} %copy-done.36, bf16[256,2048]{1,0:T(8,128)(2,1)S(1)} %copy-done.4, bf16[256,2048]{1,0:T(8,128)(2,1)S(1)} %get-tuple-element.33), kind=kOutput, calls=%fused_computation.144 | convolution fusion | flops 4307550208 | bytes 14680064 | tf_op jit(solution)/shard_map/dot_general | solution.py:20
  464.1 3.5 convolution_bitcast_fusion.1
  467.6 3.5 convolution_bitcast_fusion.2
  471.1 4.4 collective-permute-start.12
  475.5 5.0 convolution_bitcast_fusion
  480.5 7.7 %fusion.10 = bf16[1,512,1024]{2,1,0:T(8,128)(2,1)} fusion(bf16[1024,4096]{1,0:T(8,128)(2,1)S(1)} %maximum_maximum_fusion, bf16[512,2048]{1,0:T(8,128)(2,1)} %collective-permute-done.21, bf16[256,2048]{1,0:T(8,128)(2,1)} %copy-done.42, bf16[256,2048]{1,0:T(8,128)(2,1)} %get-tuple-element.24), kind=kOutput, calls=%fused_computation.46 | convolution fusion | flops 4308074496 | bytes 13631488 | tf_op jit(solution)/shard_map/dot_general | solution.py:20
  488.3 4.9 fusion.20
  493.2 4.1 fusion.26
  500.3 3.0 fusion.34
  508.9 33.1 %collective-permute-done.12 = bf16[2,512,1024]{2,1,0:T(8,128)(2,1)} collective-permute-done((bf16[2,512,1024]{2,1,0:T(8,128)(2,1)}, bf16[2,512,1024]{2,1,0:T(8,128)(2,1)}, u32[]{:S(2)}, u32[]{:S(2)}) %collective-permute-start.12) | collective-permute-done | bytes 2097184 | tf_op jit(solution)/shard_map/ppermute | solution.py:11
  544.6 26.2 %collective-permute-done.22 = bf16[2,512,1024]{2,1,0:T(8,128)(2,1)S(1)} collective-permute-done((bf16[2,512,1024]{2,1,0:T(8,128)(2,1)S(1)}, bf16[2,512,1024]{2,1,0:T(8,128)(2,1)S(1)}, u32[]{:S(2)}, u32[]{:S(2)}) %collective-permute-start.22) | collective-permute-done | bytes 2097184 | tf_op jit(solution)/shard_map/ppermute | solution.py:11
  571.2 5.0 fusion
  576.1 5.0 fusion.1
  (223 shorter events, 84.8 us)
Async XLA Ops:
  0.6 51.3 %copy-start = (bf16[1,64,2048]{2,1,0:T(8,128)(2,1)S(1)}, bf16[1,64,2048]{2,1,0:T(8,128)(2,1)}, u32[]{:S(2)}) copy-start(bf16[1,64,2048]{2,1,0:T(8,128)(2,1)} %param.10) | copy-start | bytes 786436
  0.7 48.4 %collective-permute-start.1 = (bf16[512,2048]{1,0:T(8,128)(2,1)}, bf16[512,2048]{1,0:T(8,128)(2,1)}, u32[]{:S(2)}, u32[]{:S(2)}) collective-permute-start(bf16[512,2048]{1,0:T(8,128)(2,1)} %bitcast.113), channel_id=1, source_target_pairs={{3,2},{7,6},{11,10},{15,14},{19,18},{23,22},{27,26},{31,30}} | collective-permute-start | bytes 6291464 | tf_op jit(solution)/shard_map/ppermute | solution.py:11
  4.1 24.4 %collective-permute-start.2 = (bf16[512,1024]{1,0:T(8,128)(2,1)S(1)}, bf16[512,1024]{1,0:T(8,128)(2,1)S(1)}, u32[]{:S(2)}, u32[]{:S(2)}) collective-permute-start(bf16[512,1024]{1,0:T(8,128)(2,1)S(1)} %slice.198), channel_id=1, source_target_pairs={{1,2},{5,6},{9,10},{13,14},{17,18},{21,22},{25,26},{29,30}} | collective-permute-start | bytes 3145736 | tf_op jit(solution)/shard_map/ppermute | solution.py:11
  8.3 36.9 %collective-permute-start.3 = (bf16[512,1536]{1,0:T(8,128)(2,1)S(1)}, bf16[512,1536]{1,0:T(8,128)(2,1)S(1)}, u32[]{:S(2)}, u32[]{:S(2)}) collective-permute-start(bf16[512,1536]{1,0:T(8,128)(2,1)S(1)} %slice.199), channel_id=1, source_target_pairs={{2,1},{6,5},{10,9},{14,13},{18,17},{22,21},{26,25},{30,29}} | collective-permute-start | bytes 4718600 | tf_op jit(solution)/shard_map/ppermute | solution.py:11
  10.2 10.0 %copy-start.13 = (bf16[256,2048]{1,0:T(8,128)(2,1)}, bf16[256,2048]{1,0:T(8,128)(2,1)S(1)}, u32[]{:S(2)}) copy-start(bf16[256,2048]{1,0:T(8,128)(2,1)S(1)} %get-tuple-element.53) | copy-start | bytes 3145732
  10.2 10.0 %copy-start.15 = (bf16[256,2048]{1,0:T(8,128)(2,1)}, bf16[256,2048]{1,0:T(8,128)(2,1)S(1)}, u32[]{:S(2)}) copy-start(bf16[256,2048]{1,0:T(8,128)(2,1)S(1)} %get-tuple-element.43) | copy-start | bytes 3145732
  10.2 40.2 %copy-start.2 = (bf16[1,512,2048]{2,1,0:T(8,128)(2,1)S(1)}, bf16[1,512,2048]{2,1,0:T(8,128)(2,1)}, u32[]{:S(2)}) copy-start(bf16[1,512,2048]{2,1,0:T(8,128)(2,1)} %param.7) | copy-start | bytes 6291460
  10.2 40.2 %copy-start.63 = (bf16[1,2048]{1,0:T(2,128)(2,1)S(1)}, bf16[1,2048]{1,0:T(2,128)(2,1)}, u32[]{:S(2)}) copy-start(bf16[1,2048]{1,0:T(2,128)(2,1)} %param.12) | copy-start | bytes 12292
  11.7 48.5 %collective-permute-start.9 = (bf16[512,2048]{1,0:T(8,128)(2,1)}, bf16[512,2048]{1,0:T(8,128)(2,1)}, u32[]{:S(2)}, u32[]{:S(2)}) collective-permute-start(bf16[512,2048]{1,0:T(8,128)(2,1)} %pad_maximum_fusion.6), channel_id=1, source_target_pairs={{0,1},{3,2},{4,5},{7,6},{8,9},{11,10},{12,13},{15,14},{16,17},{19,... | collective-permute-start | bytes 6291464 | tf_op jit(solution)/shard_map/ppermute | solution.py:11
  13.1 150.6 %collective-permute-start.17 = (bf16[512,2048]{1,0:T(8,128)(2,1)}, bf16[512,2048]{1,0:T(8,128)(2,1)}, u32[]{:S(2)}, u32[]{:S(2)}) collective-permute-start(bf16[512,2048]{1,0:T(8,128)(2,1)} %pad_maximum_fusion.6), channel_id=1, source_target_pairs={{1,2},{5,6},{9,10},{13,14},{17,18},{21,22},{25,26},{29,30}} | collective-permute-start | bytes 6291464 | tf_op jit(solution)/shard_map/ppermute | solution.py:11
  18.5 43.0 %copy-start.64 = (s32[256,2]{0,1:T(2,128)S(1)}, s32[256,2]{0,1:T(2,128)}, u32[]{:S(2)}) copy-start(s32[256,2]{0,1:T(2,128)} %param.13) | copy-start | bytes 6148
  28.5 20.5 %copy-start.53 = (bf16[512,1024]{1,0:T(8,128)(2,1)}, bf16[512,1024]{1,0:T(8,128)(2,1)S(1)}, u32[]{:S(2)}) copy-start(bf16[512,1024]{1,0:T(8,128)(2,1)S(1)} %collective-permute-done.2) | copy-start | bytes 3145732
  28.6 136.1 %collective-permute-start.8 = (bf16[512,2048]{1,0:T(8,128)(2,1)}, bf16[512,2048]{1,0:T(8,128)(2,1)}, u32[]{:S(2)}, u32[]{:S(2)}) collective-permute-start(bf16[512,2048]{1,0:T(8,128)(2,1)} %pad_maximum_fusion.5), channel_id=1, source_target_pairs={{0,1},{3,2},{4,5},{7,6},{8,9},{11,10},{12,13},{15,14},{16,17},{19,... | collective-permute-start | bytes 6291464 | tf_op jit(solution)/shard_map/ppermute | solution.py:11
  46.4 123.3 %collective-permute-start.13 = (bf16[512,2048]{1,0:T(8,128)(2,1)}, bf16[512,2048]{1,0:T(8,128)(2,1)}, u32[]{:S(2)}, u32[]{:S(2)}) collective-permute-start(bf16[512,2048]{1,0:T(8,128)(2,1)} %pad_maximum_fusion.5), channel_id=1, source_target_pairs={{1,2},{5,6},{9,10},{13,14},{17,18},{21,22},{25,26},{29,30}} | collective-permute-start | bytes 6291464 | tf_op jit(solution)/shard_map/ppermute | solution.py:11
  49.1 125.5 %collective-permute-start.5 = (bf16[512,2048]{1,0:T(8,128)(2,1)}, bf16[512,2048]{1,0:T(8,128)(2,1)}, u32[]{:S(2)}, u32[]{:S(2)}) collective-permute-start(bf16[512,2048]{1,0:T(8,128)(2,1)} %collective-permute-done.1), channel_id=1, source_target_pairs={{2,1},{6,5},{10,9},{14,13},{18,17},{22,21},{26,25},{30,29}} | collective-permute-start | bytes 6291464 | tf_op jit(solution)/shard_map/ppermute | solution.py:11
  60.2 112.3 %collective-permute-start = (bf16[512,512]{1,0:T(8,128)(2,1)}, bf16[512,512]{1,0:T(8,128)(2,1)}, u32[]{:S(2)}, u32[]{:S(2)}) collective-permute-start(bf16[512,512]{1,0:T(8,128)(2,1)} %slice.197), channel_id=1, source_target_pairs={{0,1},{4,5},{8,9},{12,13},{16,17},{20,21},{24,25},{28,29}} | collective-permute-start | bytes 1572872 | tf_op jit(solution)/shard_map/ppermute | solution.py:11
  163.7 88.5 %copy-start.20 = (bf16[512,2048]{1,0:T(8,128)(2,1)}, bf16[512,2048]{1,0:T(8,128)(2,1)S(1)}, u32[]{:S(2)}) copy-start(bf16[512,2048]{1,0:T(8,128)(2,1)S(1)} %pad_add_fusion.1) | copy-start | bytes 6291460
  163.7 14.9 %copy-start.16 = (bf16[256,2048]{1,0:T(8,128)(2,1)S(1)}, bf16[256,2048]{1,0:T(8,128)(2,1)}, u32[]{:S(2)}) copy-start(bf16[256,2048]{1,0:T(8,128)(2,1)} %copy-done.15) | copy-start | bytes 3145732
  163.8 14.9 %copy-start.18 = (bf16[256,2048]{1,0:T(8,128)(2,1)S(1)}, bf16[256,2048]{1,0:T(8,128)(2,1)}, u32[]{:S(2)}) copy-start(bf16[256,2048]{1,0:T(8,128)(2,1)} %copy-done.17) | copy-start | bytes 3145732
  163.8 10.8 %collective-permute-start.4 = (bf16[512,512]{1,0:T(8,128)(2,1)S(1)}, bf16[512,512]{1,0:T(8,128)(2,1)S(1)}, u32[]{:S(2)}, u32[]{:S(2)}) collective-permute-start(bf16[512,512]{1,0:T(8,128)(2,1)S(1)} %copy-done.57), channel_id=1, source_target_pairs={{0,2},{4,6},{8,10},{12,14},{16,18},{20,22},{24,26},{28,30}} | collective-permute-start | bytes 1572872 | tf_op jit(solution)/shard_map/ppermute | solution.py:11
  164.6 65.8 %collective-permute-start.18 = (bf16[512,2048]{1,0:T(8,128)(2,1)}, bf16[512,2048]{1,0:T(8,128)(2,1)}, u32[]{:S(2)}, u32[]{:S(2)}) collective-permute-start(bf16[512,2048]{1,0:T(8,128)(2,1)} %collective-permute-done.9), channel_id=1, source_target_pairs={{1,2},{5,6},{9,10},{13,14},{17,18},{21,22},{25,26},{29,30}} | collective-permute-start | bytes 6291464 | tf_op jit(solution)/shard_map/ppermute | solution.py:11
  169.7 124.5 %collective-permute-start.14 = (bf16[512,2048]{1,0:T(8,128)(2,1)}, bf16[512,2048]{1,0:T(8,128)(2,1)}, u32[]{:S(2)}, u32[]{:S(2)}) collective-permute-start(bf16[512,2048]{1,0:T(8,128)(2,1)} %collective-permute-done.8), channel_id=1, source_target_pairs={{1,2},{5,6},{9,10},{13,14},{17,18},{21,22},{25,26},{29,30}} | collective-permute-start | bytes 6291464 | tf_op jit(solution)/shard_map/ppermute | solution.py:11
  174.5 25.3 %copy-start.23 = (bf16[512,2048]{1,0:T(8,128)(2,1)}, bf16[512,2048]{1,0:T(8,128)(2,1)S(1)}, u32[]{:S(2)}) copy-start(bf16[512,2048]{1,0:T(8,128)(2,1)S(1)} %pad_add_fusion.2) | copy-start | bytes 6291460
  200.3 190.8 %copy-start.3 = (bf16[256,2048]{1,0:T(8,128)(2,1)}, bf16[256,2048]{1,0:T(8,128)(2,1)S(1)}, u32[]{:S(2)}) copy-start(bf16[256,2048]{1,0:T(8,128)(2,1)S(1)} %get-tuple-element.35) | copy-start | bytes 3145732
  215.7 229.4 %copy-start.6 = (bf16[256,2048]{1,0:T(8,128)(2,1)}, bf16[256,2048]{1,0:T(8,128)(2,1)S(1)}, u32[]{:S(2)}) copy-start(bf16[256,2048]{1,0:T(8,128)(2,1)S(1)} %get-tuple-element.39) | copy-start | bytes 3145732
  230.4 155.9 %copy-start.8 = (bf16[256,2048]{1,0:T(8,128)(2,1)}, bf16[256,2048]{1,0:T(8,128)(2,1)S(1)}, u32[]{:S(2)}) copy-start(bf16[256,2048]{1,0:T(8,128)(2,1)S(1)} %get-tuple-element.37) | copy-start | bytes 3145732
  265.9 58.6 %copy-start.42 = (bf16[256,2048]{1,0:T(8,128)(2,1)}, bf16[256,2048]{1,0:T(8,128)(2,1)S(1)}, u32[]{:S(2)}) copy-start(bf16[256,2048]{1,0:T(8,128)(2,1)S(1)} %get-tuple-element.26) | copy-start | bytes 3145732
  304.7 13.3 %copy-start.26 = (bf16[512,2048]{1,0:T(8,128)(2,1)S(1)}, bf16[512,2048]{1,0:T(8,128)(2,1)}, u32[]{:S(2)}) copy-start(bf16[512,2048]{1,0:T(8,128)(2,1)} %pad_maximum_fusion.10) | copy-start | bytes 6291460
  308.0 130.5 %copy-start.50 = (bf16[256,2048]{1,0:T(8,128)(2,1)}, bf16[256,2048]{1,0:T(8,128)(2,1)S(1)}, u32[]{:S(2)}) copy-start(bf16[256,2048]{1,0:T(8,128)(2,1)S(1)} %get-tuple-element.31) | copy-start | bytes 3145732
  308.0 23.2 %collective-permute-start.6 = (bf16[64,2048]{1,0:T(8,128)(2,1)S(1)}, bf16[64,2048]{1,0:T(8,128)(2,1)}, u32[]{:S(2)}, u32[]{:S(2)}) collective-permute-start(bf16[64,2048]{1,0:T(8,128)(2,1)S(1)} %copy-done.65), channel_id=1, source_target_pairs={{4,0},{8,4},{12,8},{16,12},{20,16},{24,20},{28,24},{5,1},{9,5},{13... | collective-permute-start | bytes 786440 | tf_op jit(solution)/shard_map/ppermute | solution.py:16
  312.6 78.6 %collective-permute-start.7 = (bf16[512,2048]{1,0:T(8,128)(2,1)S(1)}, bf16[512,2048]{1,0:T(8,128)(2,1)S(1)}, u32[]{:S(2)}, u32[]{:S(2)}) collective-permute-start(bf16[512,2048]{1,0:T(8,128)(2,1)S(1)} %copy-done.19), channel_id=1, source_target_pairs={{4,0},{8,4},{12,8},{16,12},{20,16},{24,20},{28,24},{5,1},{9,5},{13... | collective-permute-start | bytes 6291464 | tf_op jit(solution)/shard_map/ppermute | solution.py:16
  314.5 66.8 %collective-permute-start.19 = (bf16[256,2048]{1,0:T(8,128)(2,1)S(1)}, bf16[256,2048]{1,0:T(8,128)(2,1)}, u32[]{:S(2)}, u32[]{:S(2)}) collective-permute-start(bf16[256,2048]{1,0:T(8,128)(2,1)S(1)} %copy-done.54), channel_id=1, source_target_pairs={{4,0},{8,4},{12,8},{16,12},{20,16},{24,20},{28,24},{5,1},{9,5},{13... | collective-permute-start | bytes 3145736 | tf_op jit(solution)/shard_map/ppermute | solution.py:16
  318.0 55.6 %collective-permute-start.10 = (bf16[512,2048]{1,0:T(8,128)(2,1)S(1)}, bf16[512,2048]{1,0:T(8,128)(2,1)S(1)}, u32[]{:S(2)}, u32[]{:S(2)}) collective-permute-start(bf16[512,2048]{1,0:T(8,128)(2,1)S(1)} %copy-done.26), channel_id=1, source_target_pairs={{4,0},{8,4},{12,8},{16,12},{20,16},{24,20},{28,24},{5,1},{9,5},{13... | collective-permute-start | bytes 6291464 | tf_op jit(solution)/shard_map/ppermute | solution.py:16
  320.0 66.3 %collective-permute-start.15 = (bf16[256,2048]{1,0:T(8,128)(2,1)S(1)}, bf16[256,2048]{1,0:T(8,128)(2,1)}, u32[]{:S(2)}, u32[]{:S(2)}) collective-permute-start(bf16[256,2048]{1,0:T(8,128)(2,1)S(1)} %get-tuple-element.32), channel_id=1, source_target_pairs={{4,0},{8,4},{12,8},{16,12},{20,16},{24,20},{28,24},{5,1},{9,5},{13... | collective-permute-start | bytes 3145736 | tf_op jit(solution)/shard_map/ppermute | solution.py:16
  331.2 50.2 %copy-start.48 = (bf16[256,2048]{1,0:T(8,128)(2,1)S(1)}, bf16[256,2048]{1,0:T(8,128)(2,1)}, u32[]{:S(2)}) copy-start(bf16[256,2048]{1,0:T(8,128)(2,1)} %get-tuple-element.29) | copy-start | bytes 3145732
  331.2 139.8 %collective-permute-start.21 = (bf16[512,2048]{1,0:T(8,128)(2,1)}, bf16[512,2048]{1,0:T(8,128)(2,1)}, u32[]{:S(2)}, u32[]{:S(2)}) collective-permute-start(bf16[512,2048]{1,0:T(8,128)(2,1)} %pad_maximum_fusion.14), channel_id=1, source_target_pairs={{4,0},{8,4},{12,8},{16,12},{20,16},{24,20},{28,24},{5,1},{9,5},{13... | collective-permute-start | bytes 6291464 | tf_op jit(solution)/shard_map/ppermute | solution.py:16
  373.7 17.5 %copy-start.39 = (bf16[512,2048]{1,0:T(8,128)(2,1)}, bf16[512,2048]{1,0:T(8,128)(2,1)S(1)}, u32[]{:S(2)}) copy-start(bf16[512,2048]{1,0:T(8,128)(2,1)S(1)} %collective-permute-done.10) | copy-start | bytes 6291460
  376.8 121.7 %collective-permute-start.11 = (f32[64,512]{1,0:T(8,128)}, f32[64,512]{1,0:T(8,128)S(1)}, u32[]{:S(2)}, u32[]{:S(2)}) collective-permute-start(f32[64,512]{1,0:T(8,128)} %fusion.35), channel_id=1, source_target_pairs={{1,0},{2,3},{5,4},{6,7},{9,8},{10,11},{13,12},{14,15},{17,16},{18,... | collective-permute-start | bytes 393224 | tf_op jit(solution)/shard_map/ppermute | solution.py:11
  384.9 114.6 %collective-permute-start.24 = (bf16[2,512,256]{2,1,0:T(8,128)(2,1)}, bf16[2,512,256]{2,1,0:T(8,128)(2,1)}, u32[]{:S(2)}, u32[]{:S(2)}) collective-permute-start(bf16[2,512,256]{2,1,0:T(8,128)(2,1)} %pad_maximum_fusion.27), channel_id=1, source_target_pairs={{2,3},{6,7},{10,11},{14,15},{18,19},{22,23},{26,27},{30,31}} | collective-permute-start | bytes 1572872 | tf_op jit(solution)/shard_map/ppermute | solution.py:11
  389.7 113.6 %collective-permute-start.23 = (bf16[2,512,256]{2,1,0:T(8,128)(2,1)}, bf16[2,512,256]{2,1,0:T(8,128)(2,1)}, u32[]{:S(2)}, u32[]{:S(2)}) collective-permute-start(bf16[2,512,256]{2,1,0:T(8,128)(2,1)} %pad_maximum_fusion.26), channel_id=1, source_target_pairs={{2,3},{6,7},{10,11},{14,15},{18,19},{22,23},{26,27},{30,31}} | collective-permute-start | bytes 1572872 | tf_op jit(solution)/shard_map/ppermute | solution.py:11
  391.2 47.4 %copy-start.36 = (bf16[512,2048]{1,0:T(8,128)(2,1)}, bf16[512,2048]{1,0:T(8,128)(2,1)S(1)}, u32[]{:S(2)}) copy-start(bf16[512,2048]{1,0:T(8,128)(2,1)S(1)} %collective-permute-done.7) | copy-start | bytes 6291460
  443.4 63.6 %collective-permute-start.16 = (bf16[2,256,1024]{2,1,0:T(8,128)(2,1)}, bf16[2,256,1024]{2,1,0:T(8,128)(2,1)}, u32[]{:S(2)}, u32[]{:S(2)}) collective-permute-start(bf16[2,256,1024]{2,1,0:T(8,128)(2,1)} %pad_maximum_fusion.16), channel_id=1, source_target_pairs={{2,0},{6,4},{10,8},{14,12},{18,16},{22,20},{26,24},{30,28}} | collective-permute-start | bytes 3145736 | tf_op jit(solution)/shard_map/ppermute | solution.py:11
  471.1 70.9 %collective-permute-start.12 = (bf16[2,512,1024]{2,1,0:T(8,128)(2,1)}, bf16[2,512,1024]{2,1,0:T(8,128)(2,1)}, u32[]{:S(2)}, u32[]{:S(2)}) collective-permute-start(bf16[2,512,1024]{2,1,0:T(8,128)(2,1)} %pad_maximum_fusion.11), channel_id=1, source_target_pairs={{1,0},{2,3},{5,4},{6,7},{9,8},{10,11},{13,12},{14,15},{17,16},{18,... | collective-permute-start | bytes 6291464 | tf_op jit(solution)/shard_map/ppermute | solution.py:11
  498.5 9.7 %collective-permute-start.20 = (bf16[2,256,1024]{2,1,0:T(8,128)(2,1)S(1)}, bf16[2,256,1024]{2,1,0:T(8,128)(2,1)S(1)}, u32[]{:S(2)}, u32[]{:S(2)}) collective-permute-start(bf16[2,256,1024]{2,1,0:T(8,128)(2,1)S(1)} %pad_maximum_fusion.17), channel_id=1, source_target_pairs={{2,0},{6,4},{10,8},{14,12},{18,16},{22,20},{26,24},{30,28}} | collective-permute-start | bytes 3145736 | tf_op jit(solution)/shard_map/ppermute | solution.py:11
  499.5 8.8 %collective-permute-start.25 = (bf16[2,512,512]{2,1,0:T(8,128)(2,1)S(1)}, bf16[2,512,512]{2,1,0:T(8,128)(2,1)S(1)}, u32[]{:S(2)}, u32[]{:S(2)}) collective-permute-start(bf16[2,512,512]{2,1,0:T(8,128)(2,1)S(1)} %pad_maximum_fusion.18), channel_id=1, source_target_pairs={{2,3},{6,7},{10,11},{14,15},{18,19},{22,23},{26,27},{30,31}} | collective-permute-start | bytes 3145736 | tf_op jit(solution)/shard_map/ppermute | solution.py:11
  503.3 67.5 %collective-permute-start.22 = (bf16[2,512,1024]{2,1,0:T(8,128)(2,1)S(1)}, bf16[2,512,1024]{2,1,0:T(8,128)(2,1)S(1)}, u32[]{:S(2)}, u32[]{:S(2)}) collective-permute-start(bf16[2,512,1024]{2,1,0:T(8,128)(2,1)S(1)} %pad_maximum_fusion.15), channel_id=1, source_target_pairs={{2,1},{6,5},{10,9},{14,13},{18,17},{22,21},{26,25},{30,29}} | collective-permute-start | bytes 6291464 | tf_op jit(solution)/shard_map/ppermute | solution.py:11
  544.6 26.6 %copy-start.11 = (f32[1,512,512]{2,1,0:T(8,128)S(1)}, f32[1,512,512]{2,1,0:T(8,128)}, u32[]{:S(2)}) copy-start(f32[1,512,512]{2,1,0:T(8,128)} %get-tuple-element.21) | copy-start | bytes 3145732
  544.6 26.6 %copy-start.12 = (f32[1,512,512]{2,1,0:T(8,128)S(1)}, f32[1,512,512]{2,1,0:T(8,128)}, u32[]{:S(2)}) copy-start(f32[1,512,512]{2,1,0:T(8,128)} %get-tuple-element.22) | copy-start | bytes 3145732
  (46 other events, 200.5 us)

commit v2 on v1

v2 whole, which is shorter than its diff:
```python
import jax
import jax.numpy as jnp
from jax import lax
from jax.sharding import PartitionSpec as P

BF16 = jnp.bfloat16
F32 = jnp.float32


def across(value, axis, pairs):
    return lax.ppermute(value, axis, pairs)


def from_above(value):
    count = lax.axis_size("story")
    return lax.ppermute(value, "story", [(j + 1, j) for j in range(count - 1)])


def transposed(first_operand, second_operand):
    return lax.dot_general(first_operand, second_operand, (((1,), (1,)), ((), ())), preferred_element_type=F32)


def summed(value, axis):
    count = lax.axis_size(axis)
    if count & (count - 1):
        return lax.psum(value, axis)
    step = 1
    while step < count:
        value = value + lax.ppermute(value, axis, [(i, i ^ step) for i in range(count)])
        step *= 2
    return value


def drift_of(story_part, drift_pairs):
    stories = lax.axis_size("story")
    levels = jnp.arange(stories, dtype=jnp.int32)
    mine = (levels == lax.axis_index("story"))[:, None]
    work = summed(summed(jnp.where(mine, story_part[None, :], 0.0), "col"), "story")
    first_story = drift_pairs[:, 0]
    end_story = drift_pairs[:, 1]
    inside = (levels[None, :] >= first_story[:, None]) & (levels[None, :] < end_story[:, None])
    return jnp.dot(inside.astype(F32), work, precision=lax.Precision.HIGHEST)


def gathered_form(inverse, above, below, loads, sep_loads):
    share = inverse.shape[0]
    operands = jnp.concatenate([above, below, loads], 0)
    panel = transposed(operands, lax.all_gather(inverse, "col", axis=0, tiled=True))
    factors = panel[: 2 * share].astype(BF16)
    factor_above, factor_below = factors[:share], factors[share:]
    solved_half = panel[2 * share :].astype(BF16)
    whole = lax.all_gather(jnp.stack([factor_above, factor_below]), "col", axis=1, tiled=True)
    square_below = transposed(factor_below, whole[1]).astype(BF16)
    loads_below = transposed(solved_half, factor_below)
    next_square, next_loads = from_above((square_below, loads_below))
    update = transposed(factor_above, whole[0]) + next_square.astype(F32)
    coupling = -transposed(factor_above, whole[1])
    reduced = sep_loads - transposed(solved_half, factor_above) - next_loads
    return reduced, update, coupling


def middle_form(inverse, above, below, loads, sep_loads):
    share = inverse.shape[0]
    width = 4 * share
    col = lax.axis_index("col")
    right = col == 2
    to_middle = [(0, 1), (3, 2)]
    to_ends = [(1, 0), (2, 3)]

    inv_end = across(inverse, "col", to_middle)
    inv_om = across(inverse[:, : 3 * share], "col", [(1, 2), (2, 1)])
    inv_0to2 = across(inverse[:, :share], "col", [(0, 2)])
    below_end = across(below, "col", to_middle)
    below_om = across(below, "col", [(1, 2)])
    inv_3to1 = across(inv_end, "col", [(2, 1)])
    above_end = across(above, "col", to_middle)
    above_om = across(above, "col", [(1, 2)])
    below_oe, _ = lax.optimization_barrier((below_end, below_om))
    below_oe = across(below_oe, "col", [(1, 2)])
    above_oe, _ = lax.optimization_barrier((above_end, above_om))
    above_oe = across(above_oe, "col", [(1, 2)])

    inv_oe = jnp.pad(inv_0to2, ((0, 0), (0, width - share))) + inv_3to1
    inv_all = jnp.zeros((width, width), BF16)
    for place, rows in enumerate((inverse, inv_end, inv_om, inv_oe)):
        inv_all = lax.dynamic_update_slice(inv_all, rows, (place * share, 0))
    inv_all = lax.optimization_barrier(inv_all)

    def factored(rows):
        return lax.optimization_barrier(transposed(rows, inv_all).astype(BF16))

    b_own = factored(below)
    n_own = from_above(b_own)
    b_end = factored(below_end)
    n_end = from_above(b_end)
    solved_half = transposed(loads, inv_all).astype(BF16)
    next_half = from_above(solved_half)
    a_own = factored(above)
    a_end = factored(above_end)
    b_om = factored(below_om)
    n_om = from_above(b_om)
    a_om = factored(above_om)
    b_oe = factored(below_oe)
    n_oe = from_above(b_oe)
    a_oe = factored(above_oe)

    def update_of(first, second):
        return transposed(first[0], second[0]) + transposed(first[1], second[1])

    def sent(values, pairs):
        return [across(value.astype(BF16), "col", pairs).astype(F32) for value in values]

    own, end, om, oe = (a_own, n_own), (a_end, n_end), (a_om, n_om), (a_oe, n_oe)

    def returned(rows, columns, pairs):
        up = [update_of(rows[:2], column[:2]) for column in columns]
        cp = [-transposed(rows[0], column[2]) for column in columns]
        return sent(up, pairs), sent(cp, pairs)

    own, end, om, oe = own + (b_own,), end + (b_end,), om + (b_om,), oe + (b_oe,)
    near_up, near_cp = returned(end, (end, own), to_ends)
    taken_end = across(transposed(solved_half, a_end) + transposed(next_half, n_end), "col", to_ends)
    taken_own = transposed(solved_half, a_own) + transposed(next_half, n_own)
    back_om = returned(om, (own, end), [(2, 1)])
    out_om = returned(end, (om,), [(2, 3)])
    back_oe = returned(oe, (own, end), [(2, 0)])
    out_oe = returned(end, (oe,), [(2, 3)])
    mine_up = [update_of(own[:2], column[:2]) for column in (end, own, om, oe)]
    mine_cp = [-transposed(a_own, column) for column in (b_end, b_own, b_om, b_oe)]

    def assembled(which, near, mine):
        rows = (
            (near[0], near[1], back_oe[which][0], back_oe[which][1]),
            (mine[0], mine[1], back_om[which][0], back_om[which][1]),
            (mine[3], mine[2], mine[1], mine[0]),
            (out_oe[which][0], out_om[which][0], near[1], near[0]),
        )
        blocks = []
        for at in range(4):
            low = jnp.where(col == 0, rows[0][at], rows[1][at])
            high = jnp.where(right, rows[2][at], rows[3][at])
            blocks.append(jnp.where(col < 2, low, high))
        return jnp.concatenate(blocks, 1)

    update = assembled(0, near_up, mine_up)
    coupling = assembled(1, near_cp, mine_cp)
    reduced = sep_loads - jnp.where((col == 1) | right, taken_own, taken_end)
    return reduced, update, coupling


def per_device(
    inv_factor,
    coupling_above,
    coupling_below,
    interior_loads,
    separator_loads,
    lateral_pattern,
    drift_pairs,
):
    inverse = inv_factor[0]
    loads = interior_loads[0]
    solved_rows = transposed(loads, inverse)
    pattern_rows = jnp.dot(inverse, lateral_pattern[0], preferred_element_type=F32)
    story_part = jnp.dot(solved_rows, pattern_rows, precision=lax.Precision.HIGHEST)
    form = middle_form if lax.axis_size("col") == 4 else gathered_form
    reduced, update, coupling = form(inverse, coupling_above[0], coupling_below[0], loads, separator_loads[0])
    drift = drift_of(story_part, drift_pairs)
    return (solved_rows[None], reduced[None], update[None], coupling[None], drift)


def solution(mesh):
    placed = (
        P("story", "col", None),
        P("story", "col", None),
        P("story", "col", None),
        P("story", None, None),
        P("story", None, "col"),
        P("story", None),
        P(),
    )
    return jax.shard_map(
        per_device,
        mesh=mesh,
        in_specs=placed,
        out_specs=(
            P("story", None, "col"),
            P("story", None, "col"),
            P("story", "col", None),
            P("story", "col", None),
            P(),
        ),
        check_vma=False,
    )
```

time: 587 us -> 539 us (0.918)
  waiting for transfers between devices: 130 us -> 304 us
  blocking collectives: 99.1 us -> 0 us
  other arithmetic: 82.9 us -> 9.03 us
  matrix products: 178 us -> 132 us
  local copies, waits for them, and re-layouts: 27.8 us -> 12 us
  starting transfers between devices: 61.1 us -> 72.9 us
    psum x1 -> x0, blocking collectives: 99.1 us -> none  [drift_of(): work = lax.psum(jnp.where(mine, story_part[None, :], 0.0), ('story', 'col'))]
    ppermute x0 -> x5, waiting for transfers between devices: none -> 87.7 us  [summed(): lax.ppermute(value, axis, [(i, i ^ step) for i in range(count)])]
    ppermute x20 -> x27, waiting for transfers between devices: 89.8 us -> 175 us  [across(): return lax.ppermute(value, axis, pairs)]
    concatenate x6 -> x0, other arithmetic: 55.3 us -> none  [the longest x1 47.3 us: middle_form(): w_near = jnp.concatenate([w_own, w_end], 0)]
    dot_general x34 -> x50, matrix products: 177 us -> 131 us  [transposed(): lax.dot_general(first_operand, second_operand, (((1,), (1,)), ((), ())),...]
    slice x15 -> x2, local copies, waits for them, and re-layouts: 17 us -> 1.3 us  [the longest x1 1.26 us: middle_form(): inv_om = across(inverse[:, :3 * share], 'col', [(1, 2), (2, 1)])]
    dynamic_update_slice x0 -> x3, local copies, waits for them, and re-layouts: none -> 10.3 us  [middle_form(): inv_all = lax.dynamic_update_slice(inv_all, rows, (place * share, 0))]
    select_n x3, other arithmetic: 10 us -> 0.73 us  [the longest x2 0.65 us: assembled(): blocks.append(jnp.where(col < 2, low, high))]
  transfers between devices with their start and end apart: 26 -> 37, of which waited for: 6 -> 13; matrix products, arithmetic and copies ran while one was open for 44% -> 22% of each run, Pallas kernels for 0% -> 0%
where the time goes in v2:
time: 539 us; the launch traced here: 532 us
  waiting for transfers between devices  304 us (56%)
  matrix products  132 us (24%)
  starting transfers between devices  72.9 us (14%)
  local copies, waits for them, and re-layouts  12 us (2%)
  other arithmetic  9.03 us (2%)
    ppermute x27, waiting for transfers between devices, across(): return lax.ppermute(value, axis, pairs)  175 us
    dot_general x50, matrix products, transposed(): lax.dot_general(first_operand, second_operand, (((1,), (1,)), ((), ())),...  131 us
    ppermute x5, waiting for transfers between devices, summed(): lax.ppermute(value, axis, [(i, i ^ step) for i in range(count)])  87.7 us
    ppermute x27, starting transfers between devices, across(): return lax.ppermute(value, axis, pairs)  49.6 us
    ppermute x5, waiting for transfers between devices, from_above(): return lax.ppermute(value, 'story', [(j + 1, j) for j in range(count - 1)])  41.1 us
    ppermute x5, starting transfers between devices, from_above(): return lax.ppermute(value, 'story', [(j + 1, j) for j in range(count - 1)])  16.8 us
  transfers between devices with their start and end apart: 37, of which 13 were waited for; matrix products, arithmetic and copies ran while one was open for 22% of the time, Pallas kernels for 0%

profile of v2, /device:TPU:13, one launch (start us, length us, event | category | flops | bytes accessed | tf_op | source)
XLA Modules:
  0.0 532.2 jit_solution(5299994276419842341)
XLA Ops:
  3.4 4.5 collective-permute-start.11
  7.9 2.3 fusion.36
  13.4 81.1 %collective-permute-done.32 = f32[8,64]{1,0:T(8,128)S(1)} collective-permute-done((f32[8,64]{1,0:T(8,128)S(1)}, f32[8,64]{1,0:T(8,128)S(1)}, u32[]{:S(2)}, u32[]{:S(2)}) %collective-permute-start.32) | collective-permute-done | bytes 2080 | tf_op jit(solution)/shard_map/ppermute | solution.py:29
  94.8 3.2 collective-permute-done.33
  98.0 2.7 collective-permute-start.34
  104.0 4.6 collective-permute-start.13
  111.2 5.3 %collective-permute-start.1 = (bf16[512,1536]{1,0:T(8,128)(2,1)}, bf16[512,1536]{1,0:T(8,128)(2,1)}, u32[]{:S(2)}, u32[]{:S(2)}) collective-permute-start(bf16[512,1536]{1,0:T(8,128)(2,1)} %slice.16), channel_id=1, source_target_pairs={{1,2},{2,1},{5,6},{6,5},{9,10},{10,9},{13,14},{14,13},{17,18},{18,... | collective-permute-start | bytes 4718600 | tf_op jit(solution)/shard_map/ppermute | solution.py:11
  116.9 2.6 collective-permute-done.36
  119.5 3.3 collective-permute-start.12
  122.9 4.4 dynamic_update_slice.12
  128.2 23.3 %collective-permute-done.7 = bf16[512,2048]{1,0:T(8,128)(2,1)} collective-permute-done((bf16[512,2048]{1,0:T(8,128)(2,1)}, bf16[512,2048]{1,0:T(8,128)(2,1)}, u32[]{:S(2)}, u32[]{:S(2)}) %collective-permute-start.7) | collective-permute-done | bytes 2097184 | tf_op jit(solution)/shard_map/ppermute | solution.py:11
  152.2 5.1 collective-permute-start.14
  157.3 3.2 constant_dynamic-update-slice_fusion.1
  160.5 35.5 %collective-permute-done.1 = bf16[512,1536]{1,0:T(8,128)(2,1)} collective-permute-done((bf16[512,1536]{1,0:T(8,128)(2,1)}, bf16[512,1536]{1,0:T(8,128)(2,1)}, u32[]{:S(2)}, u32[]{:S(2)}) %collective-permute-start.1) | collective-permute-done | bytes 1572896 | tf_op jit(solution)/shard_map/ppermute | solution.py:11
  196.0 2.7 constant_dynamic-update-slice_fusion
  198.7 3.4 add_dynamic-update-slice_fusion
  202.1 38.8 %collective-permute-done.12 = bf16[512,2048]{1,0:T(8,128)(2,1)} collective-permute-done((bf16[512,2048]{1,0:T(8,128)(2,1)}, bf16[512,2048]{1,0:T(8,128)(2,1)}, u32[]{:S(2)}, u32[]{:S(2)}) %collective-permute-start.12) | collective-permute-done | bytes 2097184 | tf_op jit(solution)/shard_map/ppermute | solution.py:11
  240.9 8.6 %convolution_convert_fusion.3 = bf16[512,2048]{1,0:T(8,128)(2,1)S(1)} fusion(bf16[512,2048]{1,0:T(8,128)(2,1)} %collective-permute-done.12, bf16[2048,2048]{1,0:T(8,128)(2,1)} %add_dynamic-update-slice_fusion), kind=kOutput, calls=%fused_computation.5 | convolution fusion | flops 4296015872 | bytes 12582912 | tf_op jit(solution)/shard_map/dot_general | solution.py:20
  249.5 7.1 %fusion.3 = bf16[512,2048]{0,1:T(8,128)(2,1)S(1)} fusion(bf16[2048,2048]{1,0:T(8,128)(2,1)S(1)} %copy-done.2, bf16[512,2048]{1,0:T(8,128)(2,1)} %collective-permute-done.7), kind=kOutput, calls=%fused_computation.13 | convolution fusion | flops 4296015872 | bytes 12582912 | tf_op jit(solution)/shard_map/dot_general | solution.py:20
  256.6 6.4 %fusion.2 = bf16[512,2048]{0,1:T(8,128)(2,1)S(1)} fusion(bf16[2048,2048]{1,0:T(8,128)(2,1)S(1)} %copy-done.2, bf16[512,2048]{1,0:T(8,128)(2,1)} %collective-permute-done.6), kind=kOutput, calls=%fused_computation.12 | convolution fusion | flops 4296015872 | bytes 12582912 | tf_op jit(solution)/shard_map/dot_general | solution.py:20
  269.3 6.8 %fusion.4 = bf16[512,2048]{0,1:T(8,128)(2,1)S(1)} fusion(bf16[2048,2048]{1,0:T(8,128)(2,1)S(1)} %copy-done.2, bf16[512,2048]{1,0:T(8,128)(2,1)} %collective-permute-done.11), kind=kOutput, calls=%fused_computation.14 | convolution fusion | flops 4296015872 | bytes 12582912 | tf_op jit(solution)/shard_map/dot_general | solution.py:20
  279.7 2.3 fusion.56
  282.0 2.3 fusion.53
  284.3 5.0 fusion.1
  289.3 6.5 %fusion.5 = bf16[512,2048]{0,1:T(8,128)(2,1)S(1)} fusion(bf16[2048,2048]{1,0:T(8,128)(2,1)S(1)} %copy-done.2, bf16[512,2048]{1,0:T(8,128)(2,1)} %collective-permute-done.13), kind=kOutput, calls=%fused_computation.15 | convolution fusion | flops 4296015872 | bytes 12582912 | tf_op jit(solution)/shard_map/dot_general | solution.py:20
  300.0 2.7 convolution_convert_fusion.8
  302.6 5.1 fusion
  307.7 7.7 %convolution_convert_fusion.2 = bf16[512,2048]{1,0:T(8,128)(2,1)} fusion(bf16[512,2048]{1,0:T(8,128)(2,1)} %collective-permute-done.14, bf16[2048,2048]{1,0:T(8,128)(2,1)S(1)} %copy-done.2), kind=kOutput, calls=%fused_computation.4 | convolution fusion | flops 4296015872 | bytes 12582912 | tf_op jit(solution)/shard_map/dot_general | solution.py:20
  316.7 2.9 fusion.9
  320.9 2.9 convolution_negate_fusion.9
  329.9 2.3 fusion.55
  334.5 2.3 fusion.57
  339.1 6.3 %collective-permute-start.8 = (bf16[512,2048]{0,1:T(8,128)(2,1)S(1)}, bf16[512,2048]{0,1:T(8,128)(2,1)S(1)}, u32[]{:S(2)}, u32[]{:S(2)}) collective-permute-start(bf16[512,2048]{0,1:T(8,128)(2,1)S(1)} %fusion.3), channel_id=1, source_target_pairs={{4,0},{8,4},{12,8},{16,12},{20,16},{24,20},{28,24},{5,1},{9,5},{13... | collective-permute-start | bytes 6291464 | tf_op jit(solution)/shard_map/ppermute | solution.py:16
  356.5 26.3 %collective-permute-done.26 = bf16[512,512]{1,0:T(8,128)(2,1)S(1)} collective-permute-done((bf16[512,512]{1,0:T(8,128)(2,1)S(1)}, bf16[512,512]{1,0:T(8,128)(2,1)S(1)}, u32[]{:S(2)}, u32[]{:S(2)}) %collective-permute-start.26) | collective-permute-done | bytes 524320 | tf_op jit(solution)/shard_map/ppermute | solution.py:11
  384.1 3.5 collective-permute-start.24
  389.9 7.9 %collective-permute-done.31 = bf16[512,512]{1,0:T(8,128)(2,1)S(1)} collective-permute-done((bf16[512,512]{1,0:T(8,128)(2,1)S(1)}, bf16[512,512]{1,0:T(8,128)(2,1)S(1)}, u32[]{:S(2)}, u32[]{:S(2)}) %collective-permute-start.31) | collective-permute-done | bytes 524320 | tf_op jit(solution)/shard_map/ppermute | solution.py:11
  397.8 3.2 collective-permute-start.15
  403.2 3.2 collective-permute-start.4
  407.9 2.4 maximum_bitcast_fusion.1
  410.3 41.1 %collective-permute-done.4 = bf16[64,2048]{1,0:T(8,128)(2,1)S(1)} collective-permute-done((bf16[64,2048]{1,0:T(8,128)(2,1)S(1)}, bf16[64,2048]{1,0:T(8,128)(2,1)S(1)}, u32[]{:S(2)}, u32[]{:S(2)}) %collective-permute-start.4) | collective-permute-done | bytes 262176 | tf_op jit(solution)/shard_map/ppermute | solution.py:16
  458.9 2.9 fusion.17
  467.6 2.9 fusion.22
  470.6 2.8 fusion.20
  477.9 11.5 %collective-permute-done.17 = bf16[512,512]{1,0:T(8,128)(2,1)S(1)} collective-permute-done((bf16[512,512]{1,0:T(8,128)(2,1)S(1)}, bf16[512,512]{1,0:T(8,128)(2,1)S(1)}, u32[]{:S(2)}, u32[]{:S(2)}) %collective-permute-start.17) | collective-permute-done | bytes 524320 | tf_op jit(solution)/shard_map/ppermute | solution.py:11
  494.2 23.6 %collective-permute-done.21 = bf16[512,512]{1,0:T(8,128)(2,1)S(1)} collective-permute-done((bf16[512,512]{1,0:T(8,128)(2,1)S(1)}, bf16[512,512]{1,0:T(8,128)(2,1)S(1)}, u32[]{:S(2)}, u32[]{:S(2)}) %collective-permute-start.21) | collective-permute-done | bytes 524320 | tf_op jit(solution)/shard_map/ppermute | solution.py:11
  518.1 3.0 fusion.27
  521.1 7.9 %collective-permute-done.23 = bf16[512,512]{1,0:T(8,128)(2,1)S(1)} collective-permute-done((bf16[512,512]{1,0:T(8,128)(2,1)S(1)}, bf16[512,512]{1,0:T(8,128)(2,1)S(1)}, u32[]{:S(2)}, u32[]{:S(2)}) %collective-permute-start.23) | collective-permute-done | bytes 524320 | tf_op jit(solution)/shard_map/ppermute | solution.py:11
  529.4 2.4 maximum_bitcast_fusion
  (152 shorter events, 82.4 us)
Async XLA Ops:
  0.6 9.6 %copy-start.3 = (bf16[1,512,2048]{2,1,0:T(8,128)(2,1)S(1)}, bf16[1,512,2048]{2,1,0:T(8,128)(2,1)}, u32[]{:S(2)}) copy-start(bf16[1,512,2048]{2,1,0:T(8,128)(2,1)} %param.7) | copy-start | bytes 6291460
  0.7 9.6 %copy-start.15 = (bf16[1,2048]{1,0:T(2,128)(2,1)S(1)}, bf16[1,2048]{1,0:T(2,128)(2,1)}, u32[]{:S(2)}) copy-start(bf16[1,2048]{1,0:T(2,128)(2,1)} %param.12) | copy-start | bytes 12292
  0.7 108.0 %collective-permute-start = (bf16[512,2048]{1,0:T(8,128)(2,1)}, bf16[512,2048]{1,0:T(8,128)(2,1)}, u32[]{:S(2)}, u32[]{:S(2)}) collective-permute-start(bf16[512,2048]{1,0:T(8,128)(2,1)} %bitcast.145), channel_id=1, source_target_pairs={{0,1},{3,2},{4,5},{7,6},{8,9},{11,10},{12,13},{15,14},{16,17},{19,... | collective-permute-start | bytes 6291464 | tf_op jit(solution)/shard_map/ppermute | solution.py:11
  2.1 109.1 %collective-permute-start.6 = (bf16[512,2048]{1,0:T(8,128)(2,1)}, bf16[512,2048]{1,0:T(8,128)(2,1)}, u32[]{:S(2)}, u32[]{:S(2)}) collective-permute-start(bf16[512,2048]{1,0:T(8,128)(2,1)} %bitcast.155), channel_id=1, source_target_pairs={{0,1},{3,2},{4,5},{7,6},{8,9},{11,10},{12,13},{15,14},{16,17},{19,... | collective-permute-start | bytes 6291464 | tf_op jit(solution)/shard_map/ppermute | solution.py:11
  3.4 113.2 %collective-permute-start.11 = (bf16[512,2048]{1,0:T(8,128)(2,1)}, bf16[512,2048]{1,0:T(8,128)(2,1)}, u32[]{:S(2)}, u32[]{:S(2)}) collective-permute-start(bf16[512,2048]{1,0:T(8,128)(2,1)} %bitcast.156), channel_id=1, source_target_pairs={{1,2},{5,6},{9,10},{13,14},{17,18},{21,22},{25,26},{29,30}} | collective-permute-start | bytes 6291464 | tf_op jit(solution)/shard_map/ppermute | solution.py:11
  10.3 101.0 %copy-start.13 = (f32[64,512]{1,0:T(8,128)}, f32[64,512]{1,0:T(8,128)S(1)}, u32[]{:S(2)}) copy-start(f32[64,512]{1,0:T(8,128)S(1)} %fusion.36) | copy-start | bytes 393220
  11.2 83.3 %collective-permute-start.32 = (f32[8,64]{1,0:T(8,128)S(1)}, f32[8,64]{1,0:T(8,128)S(1)}, u32[]{:S(2)}, u32[]{:S(2)}) collective-permute-start(f32[8,64]{1,0:T(8,128)S(1)} %broadcast_select_fusion), channel_id=1, source_target_pairs={{0,1},{1,0},{2,3},{3,2},{4,5},{5,4},{6,7},{7,6},{8,9},{9,8},{10,11... | collective-permute-start | bytes 6152 | tf_op jit(solution)/shard_map/ppermute | solution.py:29
  94.6 3.4 collective-permute-start.33
  98.0 3.5 collective-permute-start.34
  101.5 2.5 collective-permute-start.35
  102.7 48.8 %collective-permute-start.7 = (bf16[512,2048]{1,0:T(8,128)(2,1)}, bf16[512,2048]{1,0:T(8,128)(2,1)}, u32[]{:S(2)}, u32[]{:S(2)}) collective-permute-start(bf16[512,2048]{1,0:T(8,128)(2,1)} %bitcast.153), channel_id=1, source_target_pairs={{0,1},{3,2},{4,5},{7,6},{8,9},{11,10},{12,13},{15,14},{16,17},{19,... | collective-permute-start | bytes 6291464 | tf_op jit(solution)/shard_map/ppermute | solution.py:11
  104.0 48.1 %collective-permute-start.13 = (bf16[512,2048]{1,0:T(8,128)(2,1)}, bf16[512,2048]{1,0:T(8,128)(2,1)}, u32[]{:S(2)}, u32[]{:S(2)}) collective-permute-start(bf16[512,2048]{1,0:T(8,128)(2,1)} %bitcast.154), channel_id=1, source_target_pairs={{1,2},{5,6},{9,10},{13,14},{17,18},{21,22},{25,26},{29,30}} | collective-permute-start | bytes 6291464 | tf_op jit(solution)/shard_map/ppermute | solution.py:11
  108.7 90.0 %collective-permute-start.3 = (bf16[512,2048]{1,0:T(8,128)(2,1)}, bf16[512,2048]{1,0:T(8,128)(2,1)}, u32[]{:S(2)}, u32[]{:S(2)}) collective-permute-start(bf16[512,2048]{1,0:T(8,128)(2,1)} %collective-permute-done), channel_id=1, source_target_pairs={{2,1},{6,5},{10,9},{14,13},{18,17},{22,21},{26,25},{30,29}} | collective-permute-start | bytes 6291464 | tf_op jit(solution)/shard_map/ppermute | solution.py:11
  111.2 84.7 %collective-permute-start.1 = (bf16[512,1536]{1,0:T(8,128)(2,1)}, bf16[512,1536]{1,0:T(8,128)(2,1)}, u32[]{:S(2)}, u32[]{:S(2)}) collective-permute-start(bf16[512,1536]{1,0:T(8,128)(2,1)} %slice.16), channel_id=1, source_target_pairs={{1,2},{2,1},{5,6},{6,5},{9,10},{10,9},{13,14},{14,13},{17,18},{18,... | collective-permute-start | bytes 4718600 | tf_op jit(solution)/shard_map/ppermute | solution.py:11
  116.6 2.9 collective-permute-start.36
  119.5 121.4 %collective-permute-start.12 = (bf16[512,2048]{1,0:T(8,128)(2,1)}, bf16[512,2048]{1,0:T(8,128)(2,1)}, u32[]{:S(2)}, u32[]{:S(2)}) collective-permute-start(bf16[512,2048]{1,0:T(8,128)(2,1)} %collective-permute-done.6), channel_id=1, source_target_pairs={{1,2},{5,6},{9,10},{13,14},{17,18},{21,22},{25,26},{29,30}} | collective-permute-start | bytes 6291464 | tf_op jit(solution)/shard_map/ppermute | solution.py:11
  151.5 47.2 %collective-permute-start.2 = (bf16[512,512]{1,0:T(8,128)(2,1)S(1)}, bf16[512,512]{1,0:T(8,128)(2,1)S(1)}, u32[]{:S(2)}, u32[]{:S(2)}) collective-permute-start(bf16[512,512]{1,0:T(8,128)(2,1)S(1)} %slice.17), channel_id=1, source_target_pairs={{0,2},{4,6},{8,10},{12,14},{16,18},{20,22},{24,26},{28,30}} | collective-permute-start | bytes 1572872 | tf_op jit(solution)/shard_map/ppermute | solution.py:11
  152.2 155.5 %collective-permute-start.14 = (bf16[512,2048]{1,0:T(8,128)(2,1)}, bf16[512,2048]{1,0:T(8,128)(2,1)}, u32[]{:S(2)}, u32[]{:S(2)}) collective-permute-start(bf16[512,2048]{1,0:T(8,128)(2,1)} %collective-permute-done.7), channel_id=1, source_target_pairs={{1,2},{5,6},{9,10},{13,14},{17,18},{21,22},{25,26},{29,30}} | collective-permute-start | bytes 6291464 | tf_op jit(solution)/shard_map/ppermute | solution.py:11
  202.1 47.4 %copy-start.2 = (bf16[2048,2048]{1,0:T(8,128)(2,1)S(1)}, bf16[2048,2048]{1,0:T(8,128)(2,1)}, u32[]{:S(2)}) copy-start(bf16[2048,2048]{1,0:T(8,128)(2,1)} %add_dynamic-update-slice_fusion) | copy-start | bytes 25165828
  249.5 30.2 %copy-start.22 = (bf16[512,2048]{1,0:T(8,128)(2,1)}, bf16[512,2048]{1,0:T(8,128)(2,1)S(1)}, u32[]{:S(2)}) copy-start(bf16[512,2048]{1,0:T(8,128)(2,1)S(1)} %convolution_convert_fusion.3) | copy-start | bytes 6291460
  339.1 8.9 %copy-start.11 = (bf16[512,512]{1,0:T(8,128)(2,1)S(1)}, bf16[512,512]{1,0:T(8,128)(2,1)}, u32[]{:S(2)}) copy-start(bf16[512,512]{1,0:T(8,128)(2,1)} %fusion.10) | copy-start | bytes 1572868
  339.1 10.2 %copy-start.19 = (bf16[512,512]{1,0:T(8,128)(2,1)S(1)}, bf16[512,512]{1,0:T(8,128)(2,1)}, u32[]{:S(2)}) copy-start(bf16[512,512]{1,0:T(8,128)(2,1)} %fusion.12) | copy-start | bytes 1572868
  339.1 112.3 %collective-permute-start.8 = (bf16[512,2048]{0,1:T(8,128)(2,1)S(1)}, bf16[512,2048]{0,1:T(8,128)(2,1)S(1)}, u32[]{:S(2)}, u32[]{:S(2)}) collective-permute-start(bf16[512,2048]{0,1:T(8,128)(2,1)S(1)} %fusion.3), channel_id=1, source_target_pairs={{4,0},{8,4},{12,8},{16,12},{20,16},{24,20},{28,24},{5,1},{9,5},{13... | collective-permute-start | bytes 6291464 | tf_op jit(solution)/shard_map/ppermute | solution.py:16
  345.4 5.9 %collective-permute-start.30 = (bf16[512,512]{1,0:T(8,128)(2,1)S(1)}, bf16[512,512]{1,0:T(8,128)(2,1)S(1)}, u32[]{:S(2)}, u32[]{:S(2)}) collective-permute-start(bf16[512,512]{1,0:T(8,128)(2,1)S(1)} %copy-done.20), channel_id=1, source_target_pairs={{2,0},{6,4},{10,8},{14,12},{18,16},{22,20},{26,24},{30,28}} | collective-permute-start | bytes 1572872 | tf_op jit(solution)/shard_map/ppermute | solution.py:11
  347.3 7.3 %collective-permute-start.27 = (bf16[512,512]{1,0:T(8,128)(2,1)S(1)}, bf16[512,512]{1,0:T(8,128)(2,1)S(1)}, u32[]{:S(2)}, u32[]{:S(2)}) collective-permute-start(bf16[512,512]{1,0:T(8,128)(2,1)S(1)} %fusion.11), channel_id=1, source_target_pairs={{2,3},{6,7},{10,11},{14,15},{18,19},{22,23},{26,27},{30,31}} | collective-permute-start | bytes 1572872 | tf_op jit(solution)/shard_map/ppermute | solution.py:11
  348.0 34.9 %collective-permute-start.26 = (bf16[512,512]{1,0:T(8,128)(2,1)S(1)}, bf16[512,512]{1,0:T(8,128)(2,1)S(1)}, u32[]{:S(2)}, u32[]{:S(2)}) collective-permute-start(bf16[512,512]{1,0:T(8,128)(2,1)S(1)} %copy-done.11), channel_id=1, source_target_pairs={{1,0},{2,3},{5,4},{6,7},{9,8},{10,11},{13,12},{14,15},{17,16},{18,... | collective-permute-start | bytes 1572872 | tf_op jit(solution)/shard_map/ppermute | solution.py:11
  349.3 34.8 %collective-permute-start.28 = (bf16[512,512]{1,0:T(8,128)(2,1)S(1)}, bf16[512,512]{1,0:T(8,128)(2,1)S(1)}, u32[]{:S(2)}, u32[]{:S(2)}) collective-permute-start(bf16[512,512]{1,0:T(8,128)(2,1)S(1)} %copy-done.19), channel_id=1, source_target_pairs={{2,0},{6,4},{10,8},{14,12},{18,16},{22,20},{26,24},{30,28}} | collective-permute-start | bytes 1572872 | tf_op jit(solution)/shard_map/ppermute | solution.py:11
  351.3 36.4 %collective-permute-start.29 = (bf16[512,512]{1,0:T(8,128)(2,1)S(1)}, bf16[512,512]{1,0:T(8,128)(2,1)S(1)}, u32[]{:S(2)}, u32[]{:S(2)}) collective-permute-start(bf16[512,512]{1,0:T(8,128)(2,1)S(1)} %fusion.13), channel_id=1, source_target_pairs={{2,1},{6,5},{10,9},{14,13},{18,17},{22,21},{26,25},{30,29}} | collective-permute-start | bytes 1572872 | tf_op jit(solution)/shard_map/ppermute | solution.py:11
  353.3 30.8 %copy-start.10 = (bf16[512,512]{1,0:T(8,128)(2,1)S(1)}, bf16[512,512]{1,0:T(8,128)(2,1)}, u32[]{:S(2)}) copy-start(bf16[512,512]{1,0:T(8,128)(2,1)} %fusion.8) | copy-start | bytes 1572868
  354.6 101.5 %collective-permute-start.5 = (bf16[512,2048]{0,1:T(8,128)(2,1)S(1)}, bf16[512,2048]{0,1:T(8,128)(2,1)S(1)}, u32[]{:S(2)}, u32[]{:S(2)}) collective-permute-start(bf16[512,2048]{0,1:T(8,128)(2,1)S(1)} %fusion.1), channel_id=1, source_target_pairs={{4,0},{8,4},{12,8},{16,12},{20,16},{24,20},{28,24},{5,1},{9,5},{13... | collective-permute-start | bytes 6291464 | tf_op jit(solution)/shard_map/ppermute | solution.py:16
  382.8 15.0 %collective-permute-start.31 = (bf16[512,512]{1,0:T(8,128)(2,1)S(1)}, bf16[512,512]{1,0:T(8,128)(2,1)S(1)}, u32[]{:S(2)}, u32[]{:S(2)}) collective-permute-start(bf16[512,512]{1,0:T(8,128)(2,1)S(1)} %fusion.15), channel_id=1, source_target_pairs={{2,1},{6,5},{10,9},{14,13},{18,17},{22,21},{26,25},{30,29}} | collective-permute-start | bytes 1572872 | tf_op jit(solution)/shard_map/ppermute | solution.py:11
  384.1 16.8 %collective-permute-start.24 = (bf16[512,512]{1,0:T(8,128)(2,1)S(1)}, bf16[512,512]{1,0:T(8,128)(2,1)S(1)}, u32[]{:S(2)}, u32[]{:S(2)}) collective-permute-start(bf16[512,512]{1,0:T(8,128)(2,1)S(1)} %copy-done.10), channel_id=1, source_target_pairs={{1,0},{2,3},{5,4},{6,7},{9,8},{10,11},{13,12},{14,15},{17,16},{18,... | collective-permute-start | bytes 1572872 | tf_op jit(solution)/shard_map/ppermute | solution.py:11
  387.7 15.5 %collective-permute-start.25 = (bf16[512,512]{1,0:T(8,128)(2,1)S(1)}, bf16[512,512]{1,0:T(8,128)(2,1)S(1)}, u32[]{:S(2)}, u32[]{:S(2)}) collective-permute-start(bf16[512,512]{1,0:T(8,128)(2,1)S(1)} %fusion.9), channel_id=1, source_target_pairs={{2,3},{6,7},{10,11},{14,15},{18,19},{22,23},{26,27},{30,31}} | collective-permute-start | bytes 1572872 | tf_op jit(solution)/shard_map/ppermute | solution.py:11
  397.8 61.1 %collective-permute-start.15 = (bf16[512,2048]{1,0:T(8,128)(2,1)}, bf16[512,2048]{1,0:T(8,128)(2,1)}, u32[]{:S(2)}, u32[]{:S(2)}) collective-permute-start(bf16[512,2048]{1,0:T(8,128)(2,1)} %convolution_convert_fusion.2), channel_id=1, source_target_pairs={{4,0},{8,4},{12,8},{16,12},{20,16},{24,20},{28,24},{5,1},{9,5},{13... | collective-permute-start | bytes 6291464 | tf_op jit(solution)/shard_map/ppermute | solution.py:16
  401.0 61.7 %collective-permute-start.18 = (bf16[512,2048]{0,1:T(8,128)(2,1)S(1)}, bf16[512,2048]{0,1:T(8,128)(2,1)S(1)}, u32[]{:S(2)}, u32[]{:S(2)}) collective-permute-start(bf16[512,2048]{0,1:T(8,128)(2,1)S(1)} %fusion.5), channel_id=1, source_target_pairs={{4,0},{8,4},{12,8},{16,12},{20,16},{24,20},{28,24},{5,1},{9,5},{13... | collective-permute-start | bytes 6291464 | tf_op jit(solution)/shard_map/ppermute | solution.py:16
  403.2 48.2 %collective-permute-start.4 = (bf16[64,2048]{1,0:T(8,128)(2,1)S(1)}, bf16[64,2048]{1,0:T(8,128)(2,1)S(1)}, u32[]{:S(2)}, u32[]{:S(2)}) collective-permute-start(bf16[64,2048]{1,0:T(8,128)(2,1)S(1)} %bitcast.149), channel_id=1, source_target_pairs={{4,0},{8,4},{12,8},{16,12},{20,16},{24,20},{28,24},{5,1},{9,5},{13... | collective-permute-start | bytes 786440 | tf_op jit(solution)/shard_map/ppermute | solution.py:16
  407.9 43.5 %copy-start.12 = (f32[64,512]{1,0:T(8,128)S(1)}, f32[64,512]{1,0:T(8,128)}, u32[]{:S(2)}) copy-start(f32[64,512]{1,0:T(8,128)} %fusion.52) | copy-start | bytes 393220
  410.3 43.1 %copy-start.8 = (f32[512,512]{1,0:T(8,128)S(1)}, f32[512,512]{1,0:T(8,128)}, u32[]{:S(2)}) copy-start(f32[512,512]{1,0:T(8,128)} %fusion.53) | copy-start | bytes 3145732
  451.9 24.1 %collective-permute-start.9 = (f32[64,512]{1,0:T(8,128)S(1)}, f32[64,512]{1,0:T(8,128)S(1)}, u32[]{:S(2)}, u32[]{:S(2)}) collective-permute-start(f32[64,512]{1,0:T(8,128)S(1)} %convolution_add_fusion.12), channel_id=1, source_target_pairs={{1,0},{2,3},{5,4},{6,7},{9,8},{10,11},{13,12},{14,15},{17,16},{18,... | collective-permute-start | bytes 393224 | tf_op jit(solution)/shard_map/ppermute | solution.py:11
  454.6 63.5 %collective-permute-start.10 = (bf16[512,512]{1,0:T(8,128)(2,1)S(1)}, bf16[512,512]{1,0:T(8,128)(2,1)S(1)}, u32[]{:S(2)}, u32[]{:S(2)}) collective-permute-start(bf16[512,512]{1,0:T(8,128)(2,1)S(1)} %fusion.16), channel_id=1, source_target_pairs={{1,0},{2,3},{5,4},{6,7},{9,8},{10,11},{13,12},{14,15},{17,16},{18,... | collective-permute-start | bytes 1572872 | tf_op jit(solution)/shard_map/ppermute | solution.py:11
  457.4 32.0 %collective-permute-start.17 = (bf16[512,512]{1,0:T(8,128)(2,1)S(1)}, bf16[512,512]{1,0:T(8,128)(2,1)S(1)}, u32[]{:S(2)}, u32[]{:S(2)}) collective-permute-start(bf16[512,512]{1,0:T(8,128)(2,1)S(1)} %fusion.18), channel_id=1, source_target_pairs={{1,0},{2,3},{5,4},{6,7},{9,8},{10,11},{13,12},{14,15},{17,16},{18,... | collective-permute-start | bytes 1572872 | tf_op jit(solution)/shard_map/ppermute | solution.py:11
  461.8 56.3 %collective-permute-start.16 = (bf16[512,512]{1,0:T(8,128)(2,1)S(1)}, bf16[512,512]{1,0:T(8,128)(2,1)S(1)}, u32[]{:S(2)}, u32[]{:S(2)}) collective-permute-start(bf16[512,512]{1,0:T(8,128)(2,1)S(1)} %fusion.17), channel_id=1, source_target_pairs={{2,3},{6,7},{10,11},{14,15},{18,19},{22,23},{26,27},{30,31}} | collective-permute-start | bytes 1572872 | tf_op jit(solution)/shard_map/ppermute | solution.py:11
  463.9 26.1 %collective-permute-start.19 = (bf16[512,512]{1,0:T(8,128)(2,1)S(1)}, bf16[512,512]{1,0:T(8,128)(2,1)S(1)}, u32[]{:S(2)}, u32[]{:S(2)}) collective-permute-start(bf16[512,512]{1,0:T(8,128)(2,1)S(1)} %fusion.19), channel_id=1, source_target_pairs={{2,3},{6,7},{10,11},{14,15},{18,19},{22,23},{26,27},{30,31}} | collective-permute-start | bytes 1572872 | tf_op jit(solution)/shard_map/ppermute | solution.py:11
  476.0 16.7 %collective-permute-start.20 = (bf16[512,512]{1,0:T(8,128)(2,1)S(1)}, bf16[512,512]{1,0:T(8,128)(2,1)S(1)}, u32[]{:S(2)}, u32[]{:S(2)}) collective-permute-start(bf16[512,512]{1,0:T(8,128)(2,1)S(1)} %fusion.20), channel_id=1, source_target_pairs={{2,0},{6,4},{10,8},{14,12},{18,16},{22,20},{26,24},{30,28}} | collective-permute-start | bytes 1572872 | tf_op jit(solution)/shard_map/ppermute | solution.py:11
  489.4 31.8 %collective-permute-start.22 = (bf16[512,512]{1,0:T(8,128)(2,1)S(1)}, bf16[512,512]{1,0:T(8,128)(2,1)S(1)}, u32[]{:S(2)}, u32[]{:S(2)}) collective-permute-start(bf16[512,512]{1,0:T(8,128)(2,1)S(1)} %fusion.22), channel_id=1, source_target_pairs={{2,0},{6,4},{10,8},{14,12},{18,16},{22,20},{26,24},{30,28}} | collective-permute-start | bytes 1572872 | tf_op jit(solution)/shard_map/ppermute | solution.py:11
  490.1 27.7 %collective-permute-start.21 = (bf16[512,512]{1,0:T(8,128)(2,1)S(1)}, bf16[512,512]{1,0:T(8,128)(2,1)S(1)}, u32[]{:S(2)}, u32[]{:S(2)}) collective-permute-start(bf16[512,512]{1,0:T(8,128)(2,1)S(1)} %fusion.21), channel_id=1, source_target_pairs={{2,1},{6,5},{10,9},{14,13},{18,17},{22,21},{26,25},{30,29}} | collective-permute-start | bytes 1572872 | tf_op jit(solution)/shard_map/ppermute | solution.py:11
  492.7 25.4 %copy-start.21 = (f32[512,512]{1,0:T(8,128)S(1)}, f32[512,512]{1,0:T(8,128)}, u32[]{:S(2)}) copy-start(f32[512,512]{1,0:T(8,128)} %fusion.55) | copy-start | bytes 3145732
  492.8 36.2 %collective-permute-start.23 = (bf16[512,512]{1,0:T(8,128)(2,1)S(1)}, bf16[512,512]{1,0:T(8,128)(2,1)S(1)}, u32[]{:S(2)}, u32[]{:S(2)}) collective-permute-start(bf16[512,512]{1,0:T(8,128)(2,1)S(1)} %fusion.23), channel_id=1, source_target_pairs={{2,1},{6,5},{10,9},{14,13},{18,17},{22,21},{26,25},{30,29}} | collective-permute-start | bytes 1572872 | tf_op jit(solution)/shard_map/ppermute | solution.py:11
  (17 other events, 62.6 us)

commit v3 on v2

--- a/solution.py
+++ b/solution.py
@@ -56,7 +56,7 @@
     update = transposed(factor_above, whole[0]) + next_square.astype(F32)
     coupling = -transposed(factor_above, whole[1])
     reduced = sep_loads - transposed(solved_half, factor_above) - next_loads
-    return reduced, update, coupling
+    return reduced, update, coupling, update
 
 
 def middle_form(inverse, above, below, loads, sep_loads):
@@ -89,20 +89,23 @@
     def factored(rows):
         return lax.optimization_barrier(transposed(rows, inv_all).astype(BF16))
 
+    def after(value, other):
+        return lax.optimization_barrier((value, other))[0]
+
     b_own = factored(below)
     n_own = from_above(b_own)
-    b_end = factored(below_end)
+    b_end = factored(after(below_end, b_own))
     n_end = from_above(b_end)
+    b_om = factored(after(below_om, b_end))
+    n_om = from_above(b_om)
+    b_oe = factored(after(below_oe, b_om))
+    n_oe = from_above(b_oe)
+    a_own = factored(after(above, b_oe))
     solved_half = transposed(loads, inv_all).astype(BF16)
     next_half = from_above(solved_half)
-    a_own = factored(above)
-    a_end = factored(above_end)
-    b_om = factored(below_om)
-    n_om = from_above(b_om)
-    a_om = factored(above_om)
-    b_oe = factored(below_oe)
-    n_oe = from_above(b_oe)
-    a_oe = factored(above_oe)
+    a_end = factored(after(above_end, n_own))
+    a_om = factored(after(above_om, n_end))
+    a_oe = factored(after(above_oe, n_om))
 
     def update_of(first, second):
         return transposed(first[0], second[0]) + transposed(first[1], second[1])
@@ -145,7 +148,7 @@
     update = assembled(0, near_up, mine_up)
     coupling = assembled(1, near_cp, mine_cp)
     reduced = sep_loads - jnp.where((col == 1) | right, taken_own, taken_end)
-    return reduced, update, coupling
+    return reduced, update, coupling, b_oe
 
 
 def per_device(
@@ -163,7 +166,8 @@
     pattern_rows = jnp.dot(inverse, lateral_pattern[0], preferred_element_type=F32)
     story_part = jnp.dot(solved_rows, pattern_rows, precision=lax.Precision.HIGHEST)
     form = middle_form if lax.axis_size("col") == 4 else gathered_form
-    reduced, update, coupling = form(inverse, coupling_above[0], coupling_below[0], loads, separator_loads[0])
+    reduced, update, coupling, settled = form(inverse, coupling_above[0], coupling_below[0], loads, separator_loads[0])
+    story_part, _ = lax.optimization_barrier((story_part, settled))
     drift = drift_of(story_part, drift_pairs)
     return (solved_rows[None], reduced[None], update[None], coupling[None], drift)
 

time: 539 us -> 458 us (0.85)
  the two profiles are of different devices: /device:TPU:13 before, /device:TPU:14 now
where the time goes in v3:
time: 458 us; the launch traced here: 449 us
  waiting for transfers between devices  221 us (48%)
  matrix products  142 us (31%)
  starting transfers between devices  60.5 us (13%)
  local copies, waits for them, and re-layouts  14.8 us (3%)
  other arithmetic  9.03 us (2%)
    ppermute x27, waiting for transfers between devices, across(): return lax.ppermute(value, axis, pairs)  193 us
    dot_general x50, matrix products, transposed(): lax.dot_general(first_operand, second_operand, (((1,), (1,)), ((), ())),...  140 us
    ppermute x27, starting transfers between devices, across(): return lax.ppermute(value, axis, pairs)  43.8 us
    ppermute x5, waiting for transfers between devices, summed(): lax.ppermute(value, axis, [(i, i ^ step) for i in range(count)])  27.7 us
    ppermute x5, starting transfers between devices, from_above(): return lax.ppermute(value, 'story', [(j + 1, j) for j in range(count - 1)])  11.5 us
    dynamic_update_slice x3, local copies, waits for them, and re-layouts, middle_form(): inv_all = lax.dynamic_update_slice(inv_all, rows, (place * share, 0))  10.3 us
  transfers between devices with their start and end apart: 37, of which 12 were waited for; matrix products, arithmetic and copies ran while one was open for 36% of the time, Pallas kernels for 0%

profile of v3, /device:TPU:14, one launch (start us, length us, event | category | flops | bytes accessed | tf_op | source)
XLA Modules:
  0.0 448.9 jit_solution(6725704254146013830)
XLA Ops:
  3.4 4.8 %collective-permute-start.5 = (bf16[512,2048]{1,0:T(8,128)(2,1)}, bf16[512,2048]{1,0:T(8,128)(2,1)}, u32[]{:S(2)}, u32[]{:S(2)}) collective-permute-start(bf16[512,2048]{1,0:T(8,128)(2,1)} %bitcast.143), channel_id=1, source_target_pairs={{1,2},{5,6},{9,10},{13,14},{17,18},{21,22},{25,26},{29,30}} | collective-permute-start | bytes 6291464 | tf_op jit(solution)/shard_map/ppermute | solution.py:11
  9.5 2.6 collective-permute-start.13
  12.1 39.4 %collective-permute-done = bf16[512,2048]{1,0:T(8,128)(2,1)} collective-permute-done((bf16[512,2048]{1,0:T(8,128)(2,1)}, bf16[512,2048]{1,0:T(8,128)(2,1)}, u32[]{:S(2)}, u32[]{:S(2)}) %collective-permute-start) | collective-permute-done | bytes 2097184 | tf_op jit(solution)/shard_map/ppermute | solution.py:11
  52.8 2.7 slice.16
  55.5 40.9 %collective-permute-done.4 = bf16[512,2048]{1,0:T(8,128)(2,1)S(1)} collective-permute-done((bf16[512,2048]{1,0:T(8,128)(2,1)}, bf16[512,2048]{1,0:T(8,128)(2,1)S(1)}, u32[]{:S(2)}, u32[]{:S(2)}) %collective-permute-start.4) | collective-permute-done | bytes 2097184 | tf_op jit(solution)/shard_map/ppermute | solution.py:11
  97.7 3.5 collective-permute-start.1
  101.2 4.3 dynamic_update_slice.12
  108.4 33.0 %collective-permute-done.9 = bf16[512,2048]{1,0:T(8,128)(2,1)} collective-permute-done((bf16[512,2048]{1,0:T(8,128)(2,1)}, bf16[512,2048]{1,0:T(8,128)(2,1)}, u32[]{:S(2)}, u32[]{:S(2)}) %collective-permute-start.9) | collective-permute-done | bytes 2097184 | tf_op jit(solution)/shard_map/ppermute | solution.py:11
  141.4 3.7 collective-permute-start.6
  145.1 2.6 collective-permute-start.14
  147.7 3.2 constant_dynamic-update-slice_fusion.1
  150.9 2.7 constant_dynamic-update-slice_fusion
  153.6 3.5 add_dynamic-update-slice_fusion
  157.1 9.3 %fusion = bf16[512,2048]{0,1:T(8,128)(2,1)} fusion(bf16[2048,2048]{1,0:T(8,128)(2,1)} %add_dynamic-update-slice_fusion, bf16[1,512,2048]{2,1,0:T(8,128)(2,1)S(1)} %copy-done.8), kind=kOutput, calls=%fused_computation.10 | convolution fusion | flops 4296015872 | bytes 12582912 | tf_op jit(solution)/shard_map/dot_general | solution.py:20
  168.3 5.8 %convolution_convert_fusion.6 = bf16[512,2048]{1,0:T(8,128)(2,1)} fusion(bf16[512,2048]{1,0:T(8,128)(2,1)S(1)} %copy-done.11, bf16[2048,2048]{1,0:T(8,128)(2,1)S(1)} %copy-done.2), kind=kOutput, calls=%fused_computation.8 | convolution fusion | flops 4296015872 | bytes 12582912 | tf_op jit(solution)/shard_map/dot_general | solution.py:20
  174.1 2.5 collective-permute-start.10
  176.6 7.7 %convolution_convert_fusion.5 = bf16[512,2048]{1,0:T(8,128)(2,1)} fusion(bf16[512,2048]{1,0:T(8,128)(2,1)} %collective-permute-done.5, bf16[2048,2048]{1,0:T(8,128)(2,1)S(1)} %copy-done.2), kind=kOutput, calls=%fused_computation.7 | convolution fusion | flops 4296015872 | bytes 12582912 | tf_op jit(solution)/shard_map/dot_general | solution.py:20
  186.6 8.8 %collective-permute-done.6 = bf16[512,2048]{1,0:T(8,128)(2,1)} collective-permute-done((bf16[512,2048]{1,0:T(8,128)(2,1)S(1)}, bf16[512,2048]{1,0:T(8,128)(2,1)}, u32[]{:S(2)}, u32[]{:S(2)}) %collective-permute-start.6) | collective-permute-done | bytes 2097184 | tf_op jit(solution)/shard_map/ppermute | solution.py:11
  195.4 7.6 %convolution_convert_fusion.4 = bf16[512,2048]{1,0:T(8,128)(2,1)} fusion(bf16[512,2048]{1,0:T(8,128)(2,1)} %collective-permute-done.6, bf16[2048,2048]{1,0:T(8,128)(2,1)S(1)} %copy-done.2), kind=kOutput, calls=%fused_computation.6 | convolution fusion | flops 4296015872 | bytes 12582912 | tf_op jit(solution)/shard_map/dot_general | solution.py:20
  203.1 4.8 %convolution_convert_fusion.3 = bf16[512,2048]{1,0:T(8,128)(2,1)S(1)} fusion(bf16[512,2048]{1,0:T(8,128)(2,1)S(1)} %bitcast.146, bf16[2048,2048]{1,0:T(8,128)(2,1)S(1)} %copy-done.2), kind=kOutput, calls=%fused_computation.5 | convolution fusion | flops 4296015872 | bytes 12582912 | tf_op jit(solution)/shard_map/dot_general | solution.py:20
  207.9 2.7 convolution_convert_fusion.8
  210.6 4.1 collective-permute-start.33
  217.0 23.5 %collective-permute-done.33 = f32[8,64]{1,0:T(8,128)S(1)} collective-permute-done((f32[8,64]{1,0:T(8,128)S(1)}, f32[8,64]{1,0:T(8,128)S(1)}, u32[]{:S(2)}, u32[]{:S(2)}) %collective-permute-start.33) | collective-permute-done | bytes 2080 | tf_op jit(solution)/shard_map/ppermute | solution.py:29
  240.6 3.9 convolution_negate_fusion.9
  254.5 2.9 collective-permute-start.7
  257.5 6.6 %convolution_convert_fusion.2 = bf16[512,2048]{1,0:T(8,128)(2,1)S(1)} fusion(bf16[512,2048]{1,0:T(8,128)(2,1)} %collective-permute-done.9, bf16[2048,2048]{1,0:T(8,128)(2,1)S(1)} %copy-done.2), kind=kOutput, calls=%fused_computation.4 | convolution fusion | flops 4296015872 | bytes 12582912 | tf_op jit(solution)/shard_map/dot_general | solution.py:20
  264.1 7.7 %convolution_convert_fusion.1 = bf16[512,2048]{1,0:T(8,128)(2,1)} fusion(bf16[512,2048]{1,0:T(8,128)(2,1)} %collective-permute-done.14, bf16[2048,2048]{1,0:T(8,128)(2,1)S(1)} %copy-done.2), kind=kOutput, calls=%fused_computation.3 | convolution fusion | flops 4296015872 | bytes 12582912 | tf_op jit(solution)/shard_map/dot_general | solution.py:20
  271.8 3.7 fusion.6
  275.5 2.9 fusion.5
  278.3 3.0 fusion.4
  281.4 3.6 fusion.7
  285.0 2.9 fusion.9
  287.9 7.8 %convolution_convert_fusion = bf16[512,2048]{1,0:T(8,128)(2,1)} fusion(bf16[512,2048]{1,0:T(8,128)(2,1)} %collective-permute-done.13, bf16[2048,2048]{1,0:T(8,128)(2,1)S(1)} %copy-done.2), kind=kOutput, calls=%fused_computation.2 | convolution fusion | flops 4296015872 | bytes 12582912 | tf_op jit(solution)/shard_map/dot_general | solution.py:20
  295.7 3.6 fusion.8
  299.4 2.9 fusion.10
  302.3 3.0 fusion.3
  332.3 2.9 fusion.12
  335.2 2.9 fusion.15
  339.3 3.0 fusion.17
  344.9 6.1 %collective-permute-done.11 = f32[64,512]{1,0:T(8,128)S(1)} collective-permute-done((f32[64,512]{1,0:T(8,128)S(1)}, f32[64,512]{1,0:T(8,128)S(1)}, u32[]{:S(2)}, u32[]{:S(2)}) %collective-permute-start.11) | collective-permute-done | bytes 131104 | tf_op jit(solution)/shard_map/ppermute | solution.py:11
  355.1 4.4 collective-permute-start.24
  360.2 3.1 fusion.28
  365.4 16.6 %collective-permute-done.31 = bf16[512,512]{1,0:T(8,128)(2,1)S(1)} collective-permute-done((bf16[512,512]{1,0:T(8,128)(2,1)S(1)}, bf16[512,512]{1,0:T(8,128)(2,1)S(1)}, u32[]{:S(2)}, u32[]{:S(2)}) %collective-permute-start.31) | collective-permute-done | bytes 524320 | tf_op jit(solution)/shard_map/ppermute | solution.py:11
  384.0 3.1 fusion.26
  388.5 26.2 %collective-permute-done.18 = bf16[512,512]{1,0:T(8,128)(2,1)S(1)} collective-permute-done((bf16[512,512]{1,0:T(8,128)(2,1)S(1)}, bf16[512,512]{1,0:T(8,128)(2,1)S(1)}, u32[]{:S(2)}, u32[]{:S(2)}) %collective-permute-start.18) | collective-permute-done | bytes 524320 | tf_op jit(solution)/shard_map/ppermute | solution.py:11
  420.4 2.9 collective-permute-done.21
  423.6 3.0 fusion.22
  426.6 19.2 %collective-permute-done.23 = bf16[512,512]{1,0:T(8,128)(2,1)S(1)} collective-permute-done((bf16[512,512]{1,0:T(8,128)(2,1)S(1)}, bf16[512,512]{1,0:T(8,128)(2,1)S(1)}, u32[]{:S(2)}, u32[]{:S(2)}) %collective-permute-start.23) | collective-permute-done | bytes 524320 | tf_op jit(solution)/shard_map/ppermute | solution.py:11
  (136 shorter events, 75.5 us)
Async XLA Ops:
  0.6 105.6 %copy-start = (bf16[1,64,2048]{2,1,0:T(8,128)(2,1)S(1)}, bf16[1,64,2048]{2,1,0:T(8,128)(2,1)}, u32[]{:S(2)}) copy-start(bf16[1,64,2048]{2,1,0:T(8,128)(2,1)} %param.10) | copy-start | bytes 786436
  0.6 100.5 %copy-start.3 = (bf16[1,512,2048]{2,1,0:T(8,128)(2,1)S(1)}, bf16[1,512,2048]{2,1,0:T(8,128)(2,1)}, u32[]{:S(2)}) copy-start(bf16[1,512,2048]{2,1,0:T(8,128)(2,1)} %param.7) | copy-start | bytes 6291460
  0.7 50.9 %collective-permute-start = (bf16[512,2048]{1,0:T(8,128)(2,1)}, bf16[512,2048]{1,0:T(8,128)(2,1)}, u32[]{:S(2)}, u32[]{:S(2)}) collective-permute-start(bf16[512,2048]{1,0:T(8,128)(2,1)} %bitcast.134), channel_id=1, source_target_pairs={{0,1},{3,2},{4,5},{7,6},{8,9},{11,10},{12,13},{15,14},{16,17},{19,... | collective-permute-start | bytes 6291464 | tf_op jit(solution)/shard_map/ppermute | solution.py:11
  2.1 94.3 %collective-permute-start.4 = (bf16[512,2048]{1,0:T(8,128)(2,1)}, bf16[512,2048]{1,0:T(8,128)(2,1)S(1)}, u32[]{:S(2)}, u32[]{:S(2)}) collective-permute-start(bf16[512,2048]{1,0:T(8,128)(2,1)} %bitcast.142), channel_id=1, source_target_pairs={{0,1},{3,2},{4,5},{7,6},{8,9},{11,10},{12,13},{15,14},{16,17},{19,... | collective-permute-start | bytes 6291464 | tf_op jit(solution)/shard_map/ppermute | solution.py:11
  3.4 104.3 %collective-permute-start.5 = (bf16[512,2048]{1,0:T(8,128)(2,1)}, bf16[512,2048]{1,0:T(8,128)(2,1)}, u32[]{:S(2)}, u32[]{:S(2)}) collective-permute-start(bf16[512,2048]{1,0:T(8,128)(2,1)} %bitcast.143), channel_id=1, source_target_pairs={{1,2},{5,6},{9,10},{13,14},{17,18},{21,22},{25,26},{29,30}} | collective-permute-start | bytes 6291464 | tf_op jit(solution)/shard_map/ppermute | solution.py:11
  8.2 133.2 %collective-permute-start.9 = (bf16[512,2048]{1,0:T(8,128)(2,1)}, bf16[512,2048]{1,0:T(8,128)(2,1)}, u32[]{:S(2)}, u32[]{:S(2)}) collective-permute-start(bf16[512,2048]{1,0:T(8,128)(2,1)} %bitcast.144), channel_id=1, source_target_pairs={{0,1},{3,2},{4,5},{7,6},{8,9},{11,10},{12,13},{15,14},{16,17},{19,... | collective-permute-start | bytes 6291464 | tf_op jit(solution)/shard_map/ppermute | solution.py:11
  9.5 135.6 %collective-permute-start.13 = (bf16[512,2048]{1,0:T(8,128)(2,1)}, bf16[512,2048]{1,0:T(8,128)(2,1)}, u32[]{:S(2)}, u32[]{:S(2)}) collective-permute-start(bf16[512,2048]{1,0:T(8,128)(2,1)} %bitcast.145), channel_id=1, source_target_pairs={{1,2},{5,6},{9,10},{13,14},{17,18},{21,22},{25,26},{29,30}} | collective-permute-start | bytes 6291464 | tf_op jit(solution)/shard_map/ppermute | solution.py:11
  51.5 102.1 %collective-permute-start.3 = (bf16[512,2048]{1,0:T(8,128)(2,1)}, bf16[512,2048]{1,0:T(8,128)(2,1)}, u32[]{:S(2)}, u32[]{:S(2)}) collective-permute-start(bf16[512,2048]{1,0:T(8,128)(2,1)} %collective-permute-done), channel_id=1, source_target_pairs={{2,1},{6,5},{10,9},{14,13},{18,17},{22,21},{26,25},{30,29}} | collective-permute-start | bytes 6291464 | tf_op jit(solution)/shard_map/ppermute | solution.py:11
  97.7 53.2 %collective-permute-start.1 = (bf16[512,1536]{1,0:T(8,128)(2,1)}, bf16[512,1536]{1,0:T(8,128)(2,1)}, u32[]{:S(2)}, u32[]{:S(2)}) collective-permute-start(bf16[512,1536]{1,0:T(8,128)(2,1)} %slice.16), channel_id=1, source_target_pairs={{1,2},{2,1},{5,6},{6,5},{9,10},{10,9},{13,14},{14,13},{17,18},{18,... | collective-permute-start | bytes 4718600 | tf_op jit(solution)/shard_map/ppermute | solution.py:11
  101.2 4.4 copy-start.6
  105.6 35.8 %copy-start.11 = (bf16[512,2048]{1,0:T(8,128)(2,1)S(1)}, bf16[512,2048]{1,0:T(8,128)(2,1)}, u32[]{:S(2)}) copy-start(bf16[512,2048]{1,0:T(8,128)(2,1)} %copy-done.10) | copy-start | bytes 6291460
  107.7 45.9 %collective-permute-start.2 = (bf16[512,512]{1,0:T(8,128)(2,1)S(1)}, bf16[512,512]{1,0:T(8,128)(2,1)S(1)}, u32[]{:S(2)}, u32[]{:S(2)}) collective-permute-start(bf16[512,512]{1,0:T(8,128)(2,1)S(1)} %slice.17), channel_id=1, source_target_pairs={{0,2},{4,6},{8,10},{12,14},{16,18},{20,22},{24,26},{28,30}} | collective-permute-start | bytes 1572872 | tf_op jit(solution)/shard_map/ppermute | solution.py:11
  141.4 54.0 %collective-permute-start.6 = (bf16[512,2048]{1,0:T(8,128)(2,1)S(1)}, bf16[512,2048]{1,0:T(8,128)(2,1)}, u32[]{:S(2)}, u32[]{:S(2)}) collective-permute-start(bf16[512,2048]{1,0:T(8,128)(2,1)S(1)} %copy-done.11), channel_id=1, source_target_pairs={{1,2},{5,6},{9,10},{13,14},{17,18},{21,22},{25,26},{29,30}} | collective-permute-start | bytes 6291464 | tf_op jit(solution)/shard_map/ppermute | solution.py:11
  145.1 119.0 %collective-permute-start.14 = (bf16[512,2048]{1,0:T(8,128)(2,1)}, bf16[512,2048]{1,0:T(8,128)(2,1)}, u32[]{:S(2)}, u32[]{:S(2)}) collective-permute-start(bf16[512,2048]{1,0:T(8,128)(2,1)} %collective-permute-done.9), channel_id=1, source_target_pairs={{1,2},{5,6},{9,10},{13,14},{17,18},{21,22},{25,26},{29,30}} | collective-permute-start | bytes 6291464 | tf_op jit(solution)/shard_map/ppermute | solution.py:11
  157.1 11.2 %copy-start.2 = (bf16[2048,2048]{1,0:T(8,128)(2,1)S(1)}, bf16[2048,2048]{1,0:T(8,128)(2,1)}, u32[]{:S(2)}) copy-start(bf16[2048,2048]{1,0:T(8,128)(2,1)} %add_dynamic-update-slice_fusion) | copy-start | bytes 25165828
  166.4 88.1 %collective-permute-start.8 = (bf16[512,2048]{0,1:T(8,128)(2,1)}, bf16[512,2048]{0,1:T(8,128)(2,1)S(1)}, u32[]{:S(2)}, u32[]{:S(2)}) collective-permute-start(bf16[512,2048]{0,1:T(8,128)(2,1)} %fusion), channel_id=1, source_target_pairs={{4,0},{8,4},{12,8},{16,12},{20,16},{24,20},{28,24},{5,1},{9,5},{13... | collective-permute-start | bytes 6291464 | tf_op jit(solution)/shard_map/ppermute | solution.py:16
  174.1 113.8 %collective-permute-start.10 = (bf16[512,2048]{1,0:T(8,128)(2,1)}, bf16[512,2048]{1,0:T(8,128)(2,1)S(1)}, u32[]{:S(2)}, u32[]{:S(2)}) collective-permute-start(bf16[512,2048]{1,0:T(8,128)(2,1)} %convolution_convert_fusion.6), channel_id=1, source_target_pairs={{4,0},{8,4},{12,8},{16,12},{20,16},{24,20},{28,24},{5,1},{9,5},{13... | collective-permute-start | bytes 6291464 | tf_op jit(solution)/shard_map/ppermute | solution.py:16
  184.3 18.8 %copy-start.9 = (bf16[1,512,2048]{2,1,0:T(8,128)(2,1)S(1)}, bf16[1,512,2048]{2,1,0:T(8,128)(2,1)}, u32[]{:S(2)}) copy-start(bf16[1,512,2048]{2,1,0:T(8,128)(2,1)} %param.8) | copy-start | bytes 6291460
  184.3 79.8 %collective-permute-start.15 = (bf16[512,2048]{1,0:T(8,128)(2,1)}, bf16[512,2048]{1,0:T(8,128)(2,1)S(1)}, u32[]{:S(2)}, u32[]{:S(2)}) collective-permute-start(bf16[512,2048]{1,0:T(8,128)(2,1)} %convolution_convert_fusion.5), channel_id=1, source_target_pairs={{4,0},{8,4},{12,8},{16,12},{20,16},{24,20},{28,24},{5,1},{9,5},{13... | collective-permute-start | bytes 6291464 | tf_op jit(solution)/shard_map/ppermute | solution.py:16
  203.1 7.5 %collective-permute-start.32 = (f32[8,64]{1,0:T(8,128)S(1)}, f32[8,64]{1,0:T(8,128)S(1)}, u32[]{:S(2)}, u32[]{:S(2)}) collective-permute-start(f32[8,64]{1,0:T(8,128)S(1)} %broadcast_select_fusion), channel_id=1, source_target_pairs={{0,1},{1,0},{2,3},{3,2},{4,5},{5,4},{6,7},{7,6},{8,9},{9,8},{10,11... | collective-permute-start | bytes 6152 | tf_op jit(solution)/shard_map/ppermute | solution.py:29
  207.9 6.8 %copy-start.12 = (bf16[512,2048]{1,0:T(8,128)(2,1)S(1)}, bf16[512,2048]{1,0:T(8,128)(2,1)}, u32[]{:S(2)}) copy-start(bf16[512,2048]{1,0:T(8,128)(2,1)} %convolution_convert_fusion.5) | copy-start | bytes 6291460
  210.6 29.8 %collective-permute-start.33 = (f32[8,64]{1,0:T(8,128)S(1)}, f32[8,64]{1,0:T(8,128)S(1)}, u32[]{:S(2)}, u32[]{:S(2)}) collective-permute-start(f32[8,64]{1,0:T(8,128)S(1)} %fusion.40), channel_id=1, source_target_pairs={{0,2},{1,3},{2,0},{3,1},{4,6},{5,7},{6,4},{7,5},{8,10},{9,11},{10,... | collective-permute-start | bytes 6152 | tf_op jit(solution)/shard_map/ppermute | solution.py:29
  240.6 3.9 collective-permute-start.34
  244.4 3.6 collective-permute-start.35
  248.1 3.6 collective-permute-start.36
  251.7 79.1 %collective-permute-start.16 = (bf16[512,2048]{1,0:T(8,128)(2,1)}, bf16[512,2048]{1,0:T(8,128)(2,1)}, u32[]{:S(2)}, u32[]{:S(2)}) collective-permute-start(bf16[512,2048]{1,0:T(8,128)(2,1)} %convolution_convert_fusion.4), channel_id=1, source_target_pairs={{4,0},{8,4},{12,8},{16,12},{20,16},{24,20},{28,24},{5,1},{9,5},{13... | collective-permute-start | bytes 6291464 | tf_op jit(solution)/shard_map/ppermute | solution.py:16
  254.5 69.0 %collective-permute-start.7 = (bf16[64,2048]{1,0:T(8,128)(2,1)S(1)}, bf16[64,2048]{1,0:T(8,128)(2,1)S(1)}, u32[]{:S(2)}, u32[]{:S(2)}) collective-permute-start(bf16[64,2048]{1,0:T(8,128)(2,1)S(1)} %bitcast.138), channel_id=1, source_target_pairs={{4,0},{8,4},{12,8},{16,12},{20,16},{24,20},{28,24},{5,1},{9,5},{13... | collective-permute-start | bytes 786440 | tf_op jit(solution)/shard_map/ppermute | solution.py:16
  295.7 3.6 copy-start.16
  318.7 34.2 %collective-permute-start.27 = (bf16[512,512]{1,0:T(8,128)(2,1)S(1)}, bf16[512,512]{1,0:T(8,128)(2,1)S(1)}, u32[]{:S(2)}, u32[]{:S(2)}) collective-permute-start(bf16[512,512]{1,0:T(8,128)(2,1)S(1)} %copy-done.14), channel_id=1, source_target_pairs={{2,3},{6,7},{10,11},{14,15},{18,19},{22,23},{26,27},{30,31}} | collective-permute-start | bytes 1572872 | tf_op jit(solution)/shard_map/ppermute | solution.py:11
  319.4 34.3 %collective-permute-start.28 = (bf16[512,512]{1,0:T(8,128)(2,1)S(1)}, bf16[512,512]{1,0:T(8,128)(2,1)S(1)}, u32[]{:S(2)}, u32[]{:S(2)}) collective-permute-start(bf16[512,512]{1,0:T(8,128)(2,1)S(1)} %copy-done.13), channel_id=1, source_target_pairs={{2,0},{6,4},{10,8},{14,12},{18,16},{22,20},{26,24},{30,28}} | collective-permute-start | bytes 1572872 | tf_op jit(solution)/shard_map/ppermute | solution.py:11
  320.1 34.9 %collective-permute-start.29 = (bf16[512,512]{1,0:T(8,128)(2,1)S(1)}, bf16[512,512]{1,0:T(8,128)(2,1)S(1)}, u32[]{:S(2)}, u32[]{:S(2)}) collective-permute-start(bf16[512,512]{1,0:T(8,128)(2,1)S(1)} %fusion.8), channel_id=1, source_target_pairs={{2,1},{6,5},{10,9},{14,13},{18,17},{22,21},{26,25},{30,29}} | collective-permute-start | bytes 1572872 | tf_op jit(solution)/shard_map/ppermute | solution.py:11
  323.5 36.0 %collective-permute-start.26 = (bf16[512,512]{1,0:T(8,128)(2,1)S(1)}, bf16[512,512]{1,0:T(8,128)(2,1)S(1)}, u32[]{:S(2)}, u32[]{:S(2)}) collective-permute-start(bf16[512,512]{1,0:T(8,128)(2,1)S(1)} %fusion.5), channel_id=1, source_target_pairs={{1,0},{2,3},{5,4},{6,7},{9,8},{10,11},{13,12},{14,15},{17,16},{18,... | collective-permute-start | bytes 1572872 | tf_op jit(solution)/shard_map/ppermute | solution.py:11
  330.7 20.3 %collective-permute-start.11 = (f32[64,512]{1,0:T(8,128)S(1)}, f32[64,512]{1,0:T(8,128)S(1)}, u32[]{:S(2)}, u32[]{:S(2)}) collective-permute-start(f32[64,512]{1,0:T(8,128)S(1)} %convolution_add_fusion.12), channel_id=1, source_target_pairs={{1,0},{2,3},{5,4},{6,7},{9,8},{10,11},{13,12},{14,15},{17,16},{18,... | collective-permute-start | bytes 393224 | tf_op jit(solution)/shard_map/ppermute | solution.py:11
  343.5 8.2 %copy-start.5 = (f32[1,64,512]{2,1,0:T(8,128)S(1)}, f32[1,64,512]{2,1,0:T(8,128)}, u32[]{:S(2)}) copy-start(f32[1,64,512]{2,1,0:T(8,128)} %param.11) | copy-start | bytes 393220
  344.9 15.3 %copy-start.15 = (f32[512,512]{1,0:T(8,128)S(1)}, f32[512,512]{1,0:T(8,128)}, u32[]{:S(2)}) copy-start(f32[512,512]{1,0:T(8,128)} %convolution_negate_fusion.5) | copy-start | bytes 3145732
  351.1 12.2 %collective-permute-start.25 = (bf16[512,512]{1,0:T(8,128)(2,1)S(1)}, bf16[512,512]{1,0:T(8,128)(2,1)S(1)}, u32[]{:S(2)}, u32[]{:S(2)}) collective-permute-start(bf16[512,512]{1,0:T(8,128)(2,1)S(1)} %fusion.4), channel_id=1, source_target_pairs={{2,3},{6,7},{10,11},{14,15},{18,19},{22,23},{26,27},{30,31}} | collective-permute-start | bytes 1572872 | tf_op jit(solution)/shard_map/ppermute | solution.py:11
  352.9 31.1 %copy-start.19 = (f32[512,512]{1,0:T(8,128)S(1)}, f32[512,512]{1,0:T(8,128)}, u32[]{:S(2)}) copy-start(f32[512,512]{1,0:T(8,128)} %convolution_negate_fusion.9) | copy-start | bytes 3145732
  352.9 11.7 %collective-permute-start.30 = (bf16[512,512]{1,0:T(8,128)(2,1)S(1)}, bf16[512,512]{1,0:T(8,128)(2,1)S(1)}, u32[]{:S(2)}, u32[]{:S(2)}) collective-permute-start(bf16[512,512]{1,0:T(8,128)(2,1)S(1)} %fusion.9), channel_id=1, source_target_pairs={{2,0},{6,4},{10,8},{14,12},{18,16},{22,20},{26,24},{30,28}} | collective-permute-start | bytes 1572872 | tf_op jit(solution)/shard_map/ppermute | solution.py:11
  353.8 28.2 %collective-permute-start.31 = (bf16[512,512]{1,0:T(8,128)(2,1)S(1)}, bf16[512,512]{1,0:T(8,128)(2,1)S(1)}, u32[]{:S(2)}, u32[]{:S(2)}) collective-permute-start(bf16[512,512]{1,0:T(8,128)(2,1)S(1)} %fusion.10), channel_id=1, source_target_pairs={{2,1},{6,5},{10,9},{14,13},{18,17},{22,21},{26,25},{30,29}} | collective-permute-start | bytes 1572872 | tf_op jit(solution)/shard_map/ppermute | solution.py:11
  355.1 28.3 %collective-permute-start.24 = (bf16[512,512]{1,0:T(8,128)(2,1)S(1)}, bf16[512,512]{1,0:T(8,128)(2,1)S(1)}, u32[]{:S(2)}, u32[]{:S(2)}) collective-permute-start(bf16[512,512]{1,0:T(8,128)(2,1)S(1)} %fusion.3), channel_id=1, source_target_pairs={{1,0},{2,3},{5,4},{6,7},{9,8},{10,11},{13,12},{14,15},{17,16},{18,... | collective-permute-start | bytes 1572872 | tf_op jit(solution)/shard_map/ppermute | solution.py:11
  359.5 64.1 %collective-permute-start.17 = (bf16[512,512]{1,0:T(8,128)(2,1)S(1)}, bf16[512,512]{1,0:T(8,128)(2,1)S(1)}, u32[]{:S(2)}, u32[]{:S(2)}) collective-permute-start(bf16[512,512]{1,0:T(8,128)(2,1)S(1)} %fusion.12), channel_id=1, source_target_pairs={{2,3},{6,7},{10,11},{14,15},{18,19},{22,23},{26,27},{30,31}} | collective-permute-start | bytes 1572872 | tf_op jit(solution)/shard_map/ppermute | solution.py:11
  363.3 60.3 %collective-permute-start.12 = (bf16[512,512]{1,0:T(8,128)(2,1)S(1)}, bf16[512,512]{1,0:T(8,128)(2,1)S(1)}, u32[]{:S(2)}, u32[]{:S(2)}) collective-permute-start(bf16[512,512]{1,0:T(8,128)(2,1)S(1)} %fusion.11), channel_id=1, source_target_pairs={{1,0},{2,3},{5,4},{6,7},{9,8},{10,11},{13,12},{14,15},{17,16},{18,... | collective-permute-start | bytes 1572872 | tf_op jit(solution)/shard_map/ppermute | solution.py:11
  364.7 22.5 %collective-permute-start.19 = (bf16[512,512]{1,0:T(8,128)(2,1)S(1)}, bf16[512,512]{1,0:T(8,128)(2,1)S(1)}, u32[]{:S(2)}, u32[]{:S(2)}) collective-permute-start(bf16[512,512]{1,0:T(8,128)(2,1)S(1)} %fusion.14), channel_id=1, source_target_pairs={{2,3},{6,7},{10,11},{14,15},{18,19},{22,23},{26,27},{30,31}} | collective-permute-start | bytes 1572872 | tf_op jit(solution)/shard_map/ppermute | solution.py:11
  382.0 32.6 %collective-permute-start.18 = (bf16[512,512]{1,0:T(8,128)(2,1)S(1)}, bf16[512,512]{1,0:T(8,128)(2,1)S(1)}, u32[]{:S(2)}, u32[]{:S(2)}) collective-permute-start(bf16[512,512]{1,0:T(8,128)(2,1)S(1)} %fusion.13), channel_id=1, source_target_pairs={{1,0},{2,3},{5,4},{6,7},{9,8},{10,11},{13,12},{14,15},{17,16},{18,... | collective-permute-start | bytes 1572872 | tf_op jit(solution)/shard_map/ppermute | solution.py:11
  383.3 35.8 %collective-permute-start.20 = (bf16[512,512]{1,0:T(8,128)(2,1)S(1)}, bf16[512,512]{1,0:T(8,128)(2,1)S(1)}, u32[]{:S(2)}, u32[]{:S(2)}) collective-permute-start(bf16[512,512]{1,0:T(8,128)(2,1)S(1)} %fusion.15), channel_id=1, source_target_pairs={{2,0},{6,4},{10,8},{14,12},{18,16},{22,20},{26,24},{30,28}} | collective-permute-start | bytes 1572872 | tf_op jit(solution)/shard_map/ppermute | solution.py:11
  387.2 36.2 %collective-permute-start.21 = (bf16[512,512]{1,0:T(8,128)(2,1)S(1)}, bf16[512,512]{1,0:T(8,128)(2,1)S(1)}, u32[]{:S(2)}, u32[]{:S(2)}) collective-permute-start(bf16[512,512]{1,0:T(8,128)(2,1)S(1)} %fusion.16), channel_id=1, source_target_pairs={{2,1},{6,5},{10,9},{14,13},{18,17},{22,21},{26,25},{30,29}} | collective-permute-start | bytes 1572872 | tf_op jit(solution)/shard_map/ppermute | solution.py:11
  414.6 12.0 %collective-permute-start.22 = (bf16[512,512]{1,0:T(8,128)(2,1)S(1)}, bf16[512,512]{1,0:T(8,128)(2,1)S(1)}, u32[]{:S(2)}, u32[]{:S(2)}) collective-permute-start(bf16[512,512]{1,0:T(8,128)(2,1)S(1)} %fusion.17), channel_id=1, source_target_pairs={{2,0},{6,4},{10,8},{14,12},{18,16},{22,20},{26,24},{30,28}} | collective-permute-start | bytes 1572872 | tf_op jit(solution)/shard_map/ppermute | solution.py:11
  419.1 26.7 %collective-permute-start.23 = (bf16[512,512]{1,0:T(8,128)(2,1)S(1)}, bf16[512,512]{1,0:T(8,128)(2,1)S(1)}, u32[]{:S(2)}, u32[]{:S(2)}) collective-permute-start(bf16[512,512]{1,0:T(8,128)(2,1)S(1)} %fusion.18), channel_id=1, source_target_pairs={{2,1},{6,5},{10,9},{14,13},{18,17},{22,21},{26,25},{30,29}} | collective-permute-start | bytes 1572872 | tf_op jit(solution)/shard_map/ppermute | solution.py:11
  (9 other events, 18.9 us)

commit v4 on v3

--- a/solution.py
+++ b/solution.py
@@ -73,8 +73,9 @@
     below_end = across(below, "col", to_middle)
     below_om = across(below, "col", [(1, 2)])
     inv_3to1 = across(inv_end, "col", [(2, 1)])
-    above_end = across(above, "col", to_middle)
-    above_om = across(above, "col", [(1, 2)])
+    above_later, _ = lax.optimization_barrier((above, (inv_om, inv_0to2)))
+    above_end = across(above_later, "col", to_middle)
+    above_om = across(above_later, "col", [(1, 2)])
     below_oe, _ = lax.optimization_barrier((below_end, below_om))
     below_oe = across(below_oe, "col", [(1, 2)])
     above_oe, _ = lax.optimization_barrier((above_end, above_om))

time: 458 us -> 464 us (1.013)
  starting transfers between devices: 60.5 us -> 138 us
  waiting for transfers between devices: 221 us -> 149 us
    ppermute x27, starting transfers between devices: 43.8 us -> 122 us  [across(): return lax.ppermute(value, axis, pairs)]
    ppermute x27, waiting for transfers between devices: 193 us -> 124 us  [across(): return lax.ppermute(value, axis, pairs)]
  transfers between devices with their start and end apart: 37 -> 37, of which waited for: 12 -> 11; matrix products, arithmetic and copies ran while one was open for 36% -> 36% of each run, Pallas kernels for 0% -> 0%
where the time goes in v4:
time: 464 us; the launch traced here: 455 us
  waiting for transfers between devices  149 us (32%)
  matrix products  145 us (31%)
  starting transfers between devices  138 us (30%)
  local copies, waits for them, and re-layouts  12.6 us (3%)
  other arithmetic  8.9 us (2%)
    dot_general x50, matrix products, transposed(): lax.dot_general(first_operand, second_operand, (((1,), (1,)), ((), ())),...  143 us
    ppermute x27, waiting for transfers between devices, across(): return lax.ppermute(value, axis, pairs)  124 us
    ppermute x27, starting transfers between devices, across(): return lax.ppermute(value, axis, pairs)  122 us
    ppermute x5, waiting for transfers between devices, summed(): lax.ppermute(value, axis, [(i, i ^ step) for i in range(count)])  24.3 us
    ppermute x5, starting transfers between devices, from_above(): return lax.ppermute(value, 'story', [(j + 1, j) for j in range(count - 1)])  11.4 us
    dynamic_update_slice x3, local copies, waits for them, and re-layouts, middle_form(): inv_all = lax.dynamic_update_slice(inv_all, rows, (place * share, 0))  10.3 us
  transfers between devices with their start and end apart: 37, of which 11 were waited for; matrix products, arithmetic and copies ran while one was open for 36% of the time, Pallas kernels for 0%

profile of v4, /device:TPU:14, one launch (start us, length us, event | category | flops | bytes accessed | tf_op | source)
XLA Modules:
  0.0 455.2 jit_solution(8826618544598403138)
XLA Ops:
  3.6 3.5 collective-permute-start.1
  8.4 3.7 collective-permute-start.5
  12.8 29.0 %collective-permute-done.1 = bf16[512,1536]{1,0:T(8,128)(2,1)} collective-permute-done((bf16[512,1536]{1,0:T(8,128)(2,1)S(1)}, bf16[512,1536]{1,0:T(8,128)(2,1)}, u32[]{:S(2)}, u32[]{:S(2)}) %collective-permute-start.1) | collective-permute-done | bytes 1572896 | tf_op jit(solution)/shard_map/ppermute | solution.py:11
  41.9 69.2 %collective-permute-start.13 = (bf16[512,2048]{1,0:T(8,128)(2,1)}, bf16[512,2048]{1,0:T(8,128)(2,1)}, u32[]{:S(2)}, u32[]{:S(2)}) collective-permute-start(bf16[512,2048]{1,0:T(8,128)(2,1)} %bitcast.4), channel_id=1, source_target_pairs={{1,2},{5,6},{9,10},{13,14},{17,18},{21,22},{25,26},{29,30}} | collective-permute-start | bytes 6291464 | tf_op jit(solution)/shard_map/ppermute | solution.py:11
  113.7 4.4 dynamic_update_slice.12
  120.5 6.0 %collective-permute-start.6 = (bf16[512,2048]{1,0:T(8,128)(2,1)}, bf16[512,2048]{1,0:T(8,128)(2,1)S(1)}, u32[]{:S(2)}, u32[]{:S(2)}) collective-permute-start(bf16[512,2048]{1,0:T(8,128)(2,1)} %collective-permute-done.4), channel_id=1, source_target_pairs={{1,2},{5,6},{9,10},{13,14},{17,18},{21,22},{25,26},{29,30}} | collective-permute-start | bytes 6291464 | tf_op jit(solution)/shard_map/ppermute | solution.py:11
  126.5 3.2 constant_dynamic-update-slice_fusion.1
  129.7 2.7 constant_dynamic-update-slice_fusion
  132.4 23.8 %collective-permute-done.13 = bf16[512,2048]{1,0:T(8,128)(2,1)} collective-permute-done((bf16[512,2048]{1,0:T(8,128)(2,1)}, bf16[512,2048]{1,0:T(8,128)(2,1)}, u32[]{:S(2)}, u32[]{:S(2)}) %collective-permute-start.13) | collective-permute-done | bytes 2097184 | tf_op jit(solution)/shard_map/ppermute | solution.py:11
  156.2 3.3 collective-permute-done.9
  159.5 2.6 collective-permute-start.14
  162.2 3.4 add_dynamic-update-slice_fusion
  165.6 9.3 %fusion = bf16[512,2048]{0,1:T(8,128)(2,1)} fusion(bf16[2048,2048]{1,0:T(8,128)(2,1)} %add_dynamic-update-slice_fusion, bf16[1,512,2048]{2,1,0:T(8,128)(2,1)S(1)} %copy-done.8), kind=kOutput, calls=%fused_computation.10 | convolution fusion | flops 4296015872 | bytes 12582912 | tf_op jit(solution)/shard_map/dot_general | solution.py:20
  176.8 7.6 %convolution_convert_fusion.6 = bf16[512,2048]{1,0:T(8,128)(2,1)} fusion(bf16[512,2048]{1,0:T(8,128)(2,1)} %collective-permute-done.4, bf16[2048,2048]{1,0:T(8,128)(2,1)S(1)} %copy-done.2), kind=kOutput, calls=%fused_computation.8 | convolution fusion | flops 4296015872 | bytes 12582912 | tf_op jit(solution)/shard_map/dot_general | solution.py:20
  184.4 2.5 collective-permute-start.10
  186.9 7.6 %convolution_convert_fusion.5 = bf16[512,2048]{1,0:T(8,128)(2,1)} fusion(bf16[512,2048]{1,0:T(8,128)(2,1)} %collective-permute-done.5, bf16[2048,2048]{1,0:T(8,128)(2,1)S(1)} %copy-done.2), kind=kOutput, calls=%fused_computation.7 | convolution fusion | flops 4296015872 | bytes 12582912 | tf_op jit(solution)/shard_map/dot_general | solution.py:20
  196.7 4.5 collective-permute-done.6
  201.1 5.8 %convolution_convert_fusion.4 = bf16[512,2048]{1,0:T(8,128)(2,1)} fusion(bf16[512,2048]{1,0:T(8,128)(2,1)S(1)} %collective-permute-done.6, bf16[2048,2048]{1,0:T(8,128)(2,1)S(1)} %copy-done.2), kind=kOutput, calls=%fused_computation.6 | convolution fusion | flops 4296015872 | bytes 12582912 | tf_op jit(solution)/shard_map/dot_general | solution.py:20
  207.0 6.6 %convolution_convert_fusion.3 = bf16[512,2048]{1,0:T(8,128)(2,1)S(1)} fusion(bf16[512,2048]{1,0:T(8,128)(2,1)} %bitcast.4, bf16[2048,2048]{1,0:T(8,128)(2,1)S(1)} %copy-done.2), kind=kOutput, calls=%fused_computation.5 | convolution fusion | flops 4296015872 | bytes 12582912 | tf_op jit(solution)/shard_map/dot_general | solution.py:20
  213.6 2.7 convolution_convert_fusion.8
  216.3 3.8 collective-permute-start.33
  220.2 3.8 convolution_negate_fusion.5
  224.0 20.1 %collective-permute-done.33 = f32[8,64]{1,0:T(8,128)S(1)} collective-permute-done((f32[8,64]{1,0:T(8,128)S(1)}, f32[8,64]{1,0:T(8,128)S(1)}, u32[]{:S(2)}, u32[]{:S(2)}) %collective-permute-start.33) | collective-permute-done | bytes 2080 | tf_op jit(solution)/shard_map/ppermute | solution.py:29
  244.2 3.9 convolution_negate_fusion.9
  258.2 2.9 collective-permute-start.7
  261.1 7.7 %convolution_convert_fusion.1 = bf16[512,2048]{1,0:T(8,128)(2,1)} fusion(bf16[512,2048]{1,0:T(8,128)(2,1)} %collective-permute-done.14, bf16[2048,2048]{1,0:T(8,128)(2,1)S(1)} %copy-done.2), kind=kOutput, calls=%fused_computation.3 | convolution fusion | flops 4296015872 | bytes 12582912 | tf_op jit(solution)/shard_map/dot_general | solution.py:20
  268.8 6.6 %convolution_convert_fusion.2 = bf16[512,2048]{1,0:T(8,128)(2,1)S(1)} fusion(bf16[512,2048]{1,0:T(8,128)(2,1)} %collective-permute-done.9, bf16[2048,2048]{1,0:T(8,128)(2,1)S(1)} %copy-done.2), kind=kOutput, calls=%fused_computation.4 | convolution fusion | flops 4296015872 | bytes 12582912 | tf_op jit(solution)/shard_map/dot_general | solution.py:20
  275.4 3.7 fusion.6
  279.1 3.0 fusion.5
  282.1 3.6 fusion.7
  285.7 2.9 fusion.9
  288.6 2.9 fusion.4
  291.5 7.8 %convolution_convert_fusion = bf16[512,2048]{1,0:T(8,128)(2,1)} fusion(bf16[512,2048]{1,0:T(8,128)(2,1)} %collective-permute-done.13, bf16[2048,2048]{1,0:T(8,128)(2,1)S(1)} %copy-done.2), kind=kOutput, calls=%fused_computation.2 | convolution fusion | flops 4296015872 | bytes 12582912 | tf_op jit(solution)/shard_map/dot_general | solution.py:20
  299.4 3.6 fusion.8
  303.0 2.9 fusion.10
  305.9 3.0 fusion.3
  335.9 2.9 fusion.12
  338.8 2.9 fusion.15
  342.9 3.0 fusion.17
  354.8 3.1 fusion.28
  357.9 14.4 %collective-permute-start.12 = (bf16[512,512]{1,0:T(8,128)(2,1)S(1)}, bf16[512,512]{1,0:T(8,128)(2,1)S(1)}, u32[]{:S(2)}, u32[]{:S(2)}) collective-permute-start(bf16[512,512]{1,0:T(8,128)(2,1)S(1)} %fusion.11), channel_id=1, source_target_pairs={{1,0},{2,3},{5,4},{6,7},{9,8},{10,11},{13,12},{14,15},{17,16},{18,... | collective-permute-start | bytes 1572872 | tf_op jit(solution)/shard_map/ppermute | solution.py:11
  373.0 6.3 %collective-permute-done.31 = bf16[512,512]{1,0:T(8,128)(2,1)S(1)} collective-permute-done((bf16[512,512]{1,0:T(8,128)(2,1)S(1)}, bf16[512,512]{1,0:T(8,128)(2,1)S(1)}, u32[]{:S(2)}, u32[]{:S(2)}) %collective-permute-start.31) | collective-permute-done | bytes 524320 | tf_op jit(solution)/shard_map/ppermute | solution.py:11
  381.3 3.1 fusion.26
  385.8 25.4 %collective-permute-done.18 = bf16[512,512]{1,0:T(8,128)(2,1)S(1)} collective-permute-done((bf16[512,512]{1,0:T(8,128)(2,1)S(1)}, bf16[512,512]{1,0:T(8,128)(2,1)S(1)}, u32[]{:S(2)}, u32[]{:S(2)}) %collective-permute-start.18) | collective-permute-done | bytes 524320 | tf_op jit(solution)/shard_map/ppermute | solution.py:11
  413.2 2.4 maximum_bitcast_fusion.1
  416.9 12.7 %collective-permute-done.21 = bf16[512,512]{1,0:T(8,128)(2,1)S(1)} collective-permute-done((bf16[512,512]{1,0:T(8,128)(2,1)S(1)}, bf16[512,512]{1,0:T(8,128)(2,1)S(1)}, u32[]{:S(2)}, u32[]{:S(2)}) %collective-permute-start.21) | collective-permute-done | bytes 524320 | tf_op jit(solution)/shard_map/ppermute | solution.py:11
  429.9 3.0 fusion.22
  432.9 19.2 %collective-permute-done.23 = bf16[512,512]{1,0:T(8,128)(2,1)S(1)} collective-permute-done((bf16[512,512]{1,0:T(8,128)(2,1)S(1)}, bf16[512,512]{1,0:T(8,128)(2,1)S(1)}, u32[]{:S(2)}, u32[]{:S(2)}) %collective-permute-start.23) | collective-permute-done | bytes 524320 | tf_op jit(solution)/shard_map/ppermute | solution.py:11
  (128 shorter events, 71.3 us)
Async XLA Ops:
  0.6 118.1 %copy-start = (bf16[1,64,2048]{2,1,0:T(8,128)(2,1)S(1)}, bf16[1,64,2048]{2,1,0:T(8,128)(2,1)}, u32[]{:S(2)}) copy-start(bf16[1,64,2048]{2,1,0:T(8,128)(2,1)} %param.10) | copy-start | bytes 786436
  0.6 11.4 %copy-start.3 = (bf16[1,512,2048]{2,1,0:T(8,128)(2,1)S(1)}, bf16[1,512,2048]{2,1,0:T(8,128)(2,1)}, u32[]{:S(2)}) copy-start(bf16[1,512,2048]{2,1,0:T(8,128)(2,1)} %param.7) | copy-start | bytes 6291460
  0.7 111.8 %collective-permute-start = (bf16[512,2048]{1,0:T(8,128)(2,1)}, bf16[512,2048]{1,0:T(8,128)(2,1)}, u32[]{:S(2)}, u32[]{:S(2)}) collective-permute-start(bf16[512,2048]{1,0:T(8,128)(2,1)} %bitcast.134), channel_id=1, source_target_pairs={{0,1},{3,2},{4,5},{7,6},{8,9},{11,10},{12,13},{15,14},{16,17},{19,... | collective-permute-start | bytes 6291464 | tf_op jit(solution)/shard_map/ppermute | solution.py:11
  3.6 38.3 %collective-permute-start.1 = (bf16[512,1536]{1,0:T(8,128)(2,1)S(1)}, bf16[512,1536]{1,0:T(8,128)(2,1)}, u32[]{:S(2)}, u32[]{:S(2)}) collective-permute-start(bf16[512,1536]{1,0:T(8,128)(2,1)S(1)} %slice.16), channel_id=1, source_target_pairs={{1,2},{2,1},{5,6},{6,5},{9,10},{10,9},{13,14},{14,13},{17,18},{18,... | collective-permute-start | bytes 4718600 | tf_op jit(solution)/shard_map/ppermute | solution.py:11
  7.1 113.3 %collective-permute-start.4 = (bf16[512,2048]{1,0:T(8,128)(2,1)}, bf16[512,2048]{1,0:T(8,128)(2,1)}, u32[]{:S(2)}, u32[]{:S(2)}) collective-permute-start(bf16[512,2048]{1,0:T(8,128)(2,1)} %bitcast.142), channel_id=1, source_target_pairs={{0,1},{3,2},{4,5},{7,6},{8,9},{11,10},{12,13},{15,14},{16,17},{19,... | collective-permute-start | bytes 6291464 | tf_op jit(solution)/shard_map/ppermute | solution.py:11
  8.4 112.1 %collective-permute-start.5 = (bf16[512,2048]{1,0:T(8,128)(2,1)}, bf16[512,2048]{1,0:T(8,128)(2,1)}, u32[]{:S(2)}, u32[]{:S(2)}) collective-permute-start(bf16[512,2048]{1,0:T(8,128)(2,1)} %bitcast.143), channel_id=1, source_target_pairs={{1,2},{5,6},{9,10},{13,14},{17,18},{21,22},{25,26},{29,30}} | collective-permute-start | bytes 6291464 | tf_op jit(solution)/shard_map/ppermute | solution.py:11
  12.1 0.7 collective-permute-start.2
  41.9 114.3 %collective-permute-start.13 = (bf16[512,2048]{1,0:T(8,128)(2,1)}, bf16[512,2048]{1,0:T(8,128)(2,1)}, u32[]{:S(2)}, u32[]{:S(2)}) collective-permute-start(bf16[512,2048]{1,0:T(8,128)(2,1)} %bitcast.4), channel_id=1, source_target_pairs={{1,2},{5,6},{9,10},{13,14},{17,18},{21,22},{25,26},{29,30}} | collective-permute-start | bytes 6291464 | tf_op jit(solution)/shard_map/ppermute | solution.py:11
  111.1 48.4 %collective-permute-start.9 = (bf16[512,2048]{1,0:T(8,128)(2,1)}, bf16[512,2048]{1,0:T(8,128)(2,1)}, u32[]{:S(2)}, u32[]{:S(2)}) collective-permute-start(bf16[512,2048]{1,0:T(8,128)(2,1)} %bitcast.4), channel_id=1, source_target_pairs={{0,1},{3,2},{4,5},{7,6},{8,9},{11,10},{12,13},{15,14},{16,17},{19,... | collective-permute-start | bytes 6291464 | tf_op jit(solution)/shard_map/ppermute | solution.py:11
  112.4 49.8 %collective-permute-start.3 = (bf16[512,2048]{1,0:T(8,128)(2,1)}, bf16[512,2048]{1,0:T(8,128)(2,1)}, u32[]{:S(2)}, u32[]{:S(2)}) collective-permute-start(bf16[512,2048]{1,0:T(8,128)(2,1)} %collective-permute-done), channel_id=1, source_target_pairs={{2,1},{6,5},{10,9},{14,13},{18,17},{22,21},{26,25},{30,29}} | collective-permute-start | bytes 6291464 | tf_op jit(solution)/shard_map/ppermute | solution.py:11
  113.7 4.4 copy-start.6
  120.5 80.7 %collective-permute-start.6 = (bf16[512,2048]{1,0:T(8,128)(2,1)}, bf16[512,2048]{1,0:T(8,128)(2,1)S(1)}, u32[]{:S(2)}, u32[]{:S(2)}) collective-permute-start(bf16[512,2048]{1,0:T(8,128)(2,1)} %collective-permute-done.4), channel_id=1, source_target_pairs={{1,2},{5,6},{9,10},{13,14},{17,18},{21,22},{25,26},{29,30}} | collective-permute-start | bytes 6291464 | tf_op jit(solution)/shard_map/ppermute | solution.py:11
  132.4 33.1 %copy-start.8 = (bf16[1,512,2048]{2,1,0:T(8,128)(2,1)S(1)}, bf16[1,512,2048]{2,1,0:T(8,128)(2,1)}, u32[]{:S(2)}) copy-start(bf16[1,512,2048]{2,1,0:T(8,128)(2,1)} %param.9) | copy-start | bytes 6291460
  159.5 98.6 %collective-permute-start.14 = (bf16[512,2048]{1,0:T(8,128)(2,1)}, bf16[512,2048]{1,0:T(8,128)(2,1)}, u32[]{:S(2)}, u32[]{:S(2)}) collective-permute-start(bf16[512,2048]{1,0:T(8,128)(2,1)} %collective-permute-done.9), channel_id=1, source_target_pairs={{1,2},{5,6},{9,10},{13,14},{17,18},{21,22},{25,26},{29,30}} | collective-permute-start | bytes 6291464 | tf_op jit(solution)/shard_map/ppermute | solution.py:11
  165.6 11.2 %copy-start.2 = (bf16[2048,2048]{1,0:T(8,128)(2,1)S(1)}, bf16[2048,2048]{1,0:T(8,128)(2,1)}, u32[]{:S(2)}) copy-start(bf16[2048,2048]{1,0:T(8,128)(2,1)} %add_dynamic-update-slice_fusion) | copy-start | bytes 25165828
  174.8 94.0 %collective-permute-start.8 = (bf16[512,2048]{0,1:T(8,128)(2,1)}, bf16[512,2048]{0,1:T(8,128)(2,1)S(1)}, u32[]{:S(2)}, u32[]{:S(2)}) collective-permute-start(bf16[512,2048]{0,1:T(8,128)(2,1)} %fusion), channel_id=1, source_target_pairs={{4,0},{8,4},{12,8},{16,12},{20,16},{24,20},{28,24},{5,1},{9,5},{13... | collective-permute-start | bytes 6291464 | tf_op jit(solution)/shard_map/ppermute | solution.py:16
  184.4 107.1 %collective-permute-start.10 = (bf16[512,2048]{1,0:T(8,128)(2,1)}, bf16[512,2048]{1,0:T(8,128)(2,1)S(1)}, u32[]{:S(2)}, u32[]{:S(2)}) collective-permute-start(bf16[512,2048]{1,0:T(8,128)(2,1)} %convolution_convert_fusion.6), channel_id=1, source_target_pairs={{4,0},{8,4},{12,8},{16,12},{20,16},{24,20},{28,24},{5,1},{9,5},{13... | collective-permute-start | bytes 6291464 | tf_op jit(solution)/shard_map/ppermute | solution.py:16
  194.5 66.6 %collective-permute-start.15 = (bf16[512,2048]{1,0:T(8,128)(2,1)}, bf16[512,2048]{1,0:T(8,128)(2,1)S(1)}, u32[]{:S(2)}, u32[]{:S(2)}) collective-permute-start(bf16[512,2048]{1,0:T(8,128)(2,1)} %convolution_convert_fusion.5), channel_id=1, source_target_pairs={{4,0},{8,4},{12,8},{16,12},{20,16},{24,20},{28,24},{5,1},{9,5},{13... | collective-permute-start | bytes 6291464 | tf_op jit(solution)/shard_map/ppermute | solution.py:16
  207.0 9.3 %collective-permute-start.32 = (f32[8,64]{1,0:T(8,128)S(1)}, f32[8,64]{1,0:T(8,128)S(1)}, u32[]{:S(2)}, u32[]{:S(2)}) collective-permute-start(f32[8,64]{1,0:T(8,128)S(1)} %broadcast_select_fusion), channel_id=1, source_target_pairs={{0,1},{1,0},{2,3},{3,2},{4,5},{5,4},{6,7},{7,6},{8,9},{9,8},{10,11... | collective-permute-start | bytes 6152 | tf_op jit(solution)/shard_map/ppermute | solution.py:29
  216.3 27.8 %collective-permute-start.33 = (f32[8,64]{1,0:T(8,128)S(1)}, f32[8,64]{1,0:T(8,128)S(1)}, u32[]{:S(2)}, u32[]{:S(2)}) collective-permute-start(f32[8,64]{1,0:T(8,128)S(1)} %fusion.40), channel_id=1, source_target_pairs={{0,2},{1,3},{2,0},{3,1},{4,6},{5,7},{6,4},{7,5},{8,10},{9,11},{10,... | collective-permute-start | bytes 6152 | tf_op jit(solution)/shard_map/ppermute | solution.py:29
  244.2 3.9 collective-permute-start.34
  248.1 3.6 collective-permute-start.35
  251.7 3.6 collective-permute-start.36
  255.3 79.0 %collective-permute-start.16 = (bf16[512,2048]{1,0:T(8,128)(2,1)}, bf16[512,2048]{1,0:T(8,128)(2,1)}, u32[]{:S(2)}, u32[]{:S(2)}) collective-permute-start(bf16[512,2048]{1,0:T(8,128)(2,1)} %convolution_convert_fusion.4), channel_id=1, source_target_pairs={{4,0},{8,4},{12,8},{16,12},{20,16},{24,20},{28,24},{5,1},{9,5},{13... | collective-permute-start | bytes 6291464 | tf_op jit(solution)/shard_map/ppermute | solution.py:16
  258.2 68.9 %collective-permute-start.7 = (bf16[64,2048]{1,0:T(8,128)(2,1)S(1)}, bf16[64,2048]{1,0:T(8,128)(2,1)S(1)}, u32[]{:S(2)}, u32[]{:S(2)}) collective-permute-start(bf16[64,2048]{1,0:T(8,128)(2,1)S(1)} %bitcast.138), channel_id=1, source_target_pairs={{4,0},{8,4},{12,8},{16,12},{20,16},{24,20},{28,24},{5,1},{9,5},{13... | collective-permute-start | bytes 786440 | tf_op jit(solution)/shard_map/ppermute | solution.py:16
  279.1 3.0 copy-start.13
  299.3 3.6 copy-start.12
  305.9 3.0 copy-start.14
  322.3 28.2 %collective-permute-start.28 = (bf16[512,512]{1,0:T(8,128)(2,1)S(1)}, bf16[512,512]{1,0:T(8,128)(2,1)S(1)}, u32[]{:S(2)}, u32[]{:S(2)}) collective-permute-start(bf16[512,512]{1,0:T(8,128)(2,1)S(1)} %copy-done.10), channel_id=1, source_target_pairs={{2,0},{6,4},{10,8},{14,12},{18,16},{22,20},{26,24},{30,28}} | collective-permute-start | bytes 1572872 | tf_op jit(solution)/shard_map/ppermute | solution.py:11
  323.0 28.4 %collective-permute-start.27 = (bf16[512,512]{1,0:T(8,128)(2,1)S(1)}, bf16[512,512]{1,0:T(8,128)(2,1)S(1)}, u32[]{:S(2)}, u32[]{:S(2)}) collective-permute-start(bf16[512,512]{1,0:T(8,128)(2,1)S(1)} %copy-done.9), channel_id=1, source_target_pairs={{2,3},{6,7},{10,11},{14,15},{18,19},{22,23},{26,27},{30,31}} | collective-permute-start | bytes 1572872 | tf_op jit(solution)/shard_map/ppermute | solution.py:11
  323.7 29.0 %collective-permute-start.29 = (bf16[512,512]{1,0:T(8,128)(2,1)S(1)}, bf16[512,512]{1,0:T(8,128)(2,1)S(1)}, u32[]{:S(2)}, u32[]{:S(2)}) collective-permute-start(bf16[512,512]{1,0:T(8,128)(2,1)S(1)} %fusion.8), channel_id=1, source_target_pairs={{2,1},{6,5},{10,9},{14,13},{18,17},{22,21},{26,25},{30,29}} | collective-permute-start | bytes 1572872 | tf_op jit(solution)/shard_map/ppermute | solution.py:11
  327.1 26.9 %collective-permute-start.26 = (bf16[512,512]{1,0:T(8,128)(2,1)S(1)}, bf16[512,512]{1,0:T(8,128)(2,1)S(1)}, u32[]{:S(2)}, u32[]{:S(2)}) collective-permute-start(bf16[512,512]{1,0:T(8,128)(2,1)S(1)} %fusion.5), channel_id=1, source_target_pairs={{1,0},{2,3},{5,4},{6,7},{9,8},{10,11},{13,12},{14,15},{17,16},{18,... | collective-permute-start | bytes 1572872 | tf_op jit(solution)/shard_map/ppermute | solution.py:11
  334.3 14.2 %collective-permute-start.11 = (f32[64,512]{1,0:T(8,128)S(1)}, f32[64,512]{1,0:T(8,128)S(1)}, u32[]{:S(2)}, u32[]{:S(2)}) collective-permute-start(f32[64,512]{1,0:T(8,128)S(1)} %convolution_add_fusion.12), channel_id=1, source_target_pairs={{1,0},{2,3},{5,4},{6,7},{9,8},{10,11},{13,12},{14,15},{17,16},{18,... | collective-permute-start | bytes 393224 | tf_op jit(solution)/shard_map/ppermute | solution.py:11
  348.6 6.2 %copy-start.11 = (f32[512,512]{1,0:T(8,128)S(1)}, f32[512,512]{1,0:T(8,128)}, u32[]{:S(2)}) copy-start(f32[512,512]{1,0:T(8,128)} %convolution_negate_fusion.5) | copy-start | bytes 3145732
  348.6 9.3 %collective-permute-start.30 = (bf16[512,512]{1,0:T(8,128)(2,1)S(1)}, bf16[512,512]{1,0:T(8,128)(2,1)S(1)}, u32[]{:S(2)}, u32[]{:S(2)}) collective-permute-start(bf16[512,512]{1,0:T(8,128)(2,1)S(1)} %fusion.9), channel_id=1, source_target_pairs={{2,0},{6,4},{10,8},{14,12},{18,16},{22,20},{26,24},{30,28}} | collective-permute-start | bytes 1572872 | tf_op jit(solution)/shard_map/ppermute | solution.py:11
  350.6 30.8 %copy-start.15 = (f32[512,512]{1,0:T(8,128)S(1)}, f32[512,512]{1,0:T(8,128)}, u32[]{:S(2)}) copy-start(f32[512,512]{1,0:T(8,128)} %convolution_negate_fusion.9) | copy-start | bytes 3145732
  350.6 21.7 %collective-permute-start.25 = (bf16[512,512]{1,0:T(8,128)(2,1)S(1)}, bf16[512,512]{1,0:T(8,128)(2,1)S(1)}, u32[]{:S(2)}, u32[]{:S(2)}) collective-permute-start(bf16[512,512]{1,0:T(8,128)(2,1)S(1)} %fusion.4), channel_id=1, source_target_pairs={{2,3},{6,7},{10,11},{14,15},{18,19},{22,23},{26,27},{30,31}} | collective-permute-start | bytes 1572872 | tf_op jit(solution)/shard_map/ppermute | solution.py:11
  351.4 27.9 %collective-permute-start.31 = (bf16[512,512]{1,0:T(8,128)(2,1)S(1)}, bf16[512,512]{1,0:T(8,128)(2,1)S(1)}, u32[]{:S(2)}, u32[]{:S(2)}) collective-permute-start(bf16[512,512]{1,0:T(8,128)(2,1)S(1)} %fusion.10), channel_id=1, source_target_pairs={{2,1},{6,5},{10,9},{14,13},{18,17},{22,21},{26,25},{30,29}} | collective-permute-start | bytes 1572872 | tf_op jit(solution)/shard_map/ppermute | solution.py:11
  352.7 27.9 %collective-permute-start.24 = (bf16[512,512]{1,0:T(8,128)(2,1)S(1)}, bf16[512,512]{1,0:T(8,128)(2,1)S(1)}, u32[]{:S(2)}, u32[]{:S(2)}) collective-permute-start(bf16[512,512]{1,0:T(8,128)(2,1)S(1)} %fusion.3), channel_id=1, source_target_pairs={{1,0},{2,3},{5,4},{6,7},{9,8},{10,11},{13,12},{14,15},{17,16},{18,... | collective-permute-start | bytes 1572872 | tf_op jit(solution)/shard_map/ppermute | solution.py:11
  354.1 75.8 %collective-permute-start.17 = (bf16[512,512]{1,0:T(8,128)(2,1)S(1)}, bf16[512,512]{1,0:T(8,128)(2,1)S(1)}, u32[]{:S(2)}, u32[]{:S(2)}) collective-permute-start(bf16[512,512]{1,0:T(8,128)(2,1)S(1)} %fusion.12), channel_id=1, source_target_pairs={{2,3},{6,7},{10,11},{14,15},{18,19},{22,23},{26,27},{30,31}} | collective-permute-start | bytes 1572872 | tf_op jit(solution)/shard_map/ppermute | solution.py:11
  357.9 72.0 %collective-permute-start.12 = (bf16[512,512]{1,0:T(8,128)(2,1)S(1)}, bf16[512,512]{1,0:T(8,128)(2,1)S(1)}, u32[]{:S(2)}, u32[]{:S(2)}) collective-permute-start(bf16[512,512]{1,0:T(8,128)(2,1)S(1)} %fusion.11), channel_id=1, source_target_pairs={{1,0},{2,3},{5,4},{6,7},{9,8},{10,11},{13,12},{14,15},{17,16},{18,... | collective-permute-start | bytes 1572872 | tf_op jit(solution)/shard_map/ppermute | solution.py:11
  372.3 12.2 %collective-permute-start.19 = (bf16[512,512]{1,0:T(8,128)(2,1)S(1)}, bf16[512,512]{1,0:T(8,128)(2,1)S(1)}, u32[]{:S(2)}, u32[]{:S(2)}) collective-permute-start(bf16[512,512]{1,0:T(8,128)(2,1)S(1)} %fusion.14), channel_id=1, source_target_pairs={{2,3},{6,7},{10,11},{14,15},{18,19},{22,23},{26,27},{30,31}} | collective-permute-start | bytes 1572872 | tf_op jit(solution)/shard_map/ppermute | solution.py:11
  379.3 31.9 %collective-permute-start.18 = (bf16[512,512]{1,0:T(8,128)(2,1)S(1)}, bf16[512,512]{1,0:T(8,128)(2,1)S(1)}, u32[]{:S(2)}, u32[]{:S(2)}) collective-permute-start(bf16[512,512]{1,0:T(8,128)(2,1)S(1)} %fusion.13), channel_id=1, source_target_pairs={{1,0},{2,3},{5,4},{6,7},{9,8},{10,11},{13,12},{14,15},{17,16},{18,... | collective-permute-start | bytes 1572872 | tf_op jit(solution)/shard_map/ppermute | solution.py:11
  380.6 35.0 %collective-permute-start.20 = (bf16[512,512]{1,0:T(8,128)(2,1)S(1)}, bf16[512,512]{1,0:T(8,128)(2,1)S(1)}, u32[]{:S(2)}, u32[]{:S(2)}) collective-permute-start(bf16[512,512]{1,0:T(8,128)(2,1)S(1)} %fusion.15), channel_id=1, source_target_pairs={{2,0},{6,4},{10,8},{14,12},{18,16},{22,20},{26,24},{30,28}} | collective-permute-start | bytes 1572872 | tf_op jit(solution)/shard_map/ppermute | solution.py:11
  384.5 45.2 %collective-permute-start.21 = (bf16[512,512]{1,0:T(8,128)(2,1)S(1)}, bf16[512,512]{1,0:T(8,128)(2,1)S(1)}, u32[]{:S(2)}, u32[]{:S(2)}) collective-permute-start(bf16[512,512]{1,0:T(8,128)(2,1)S(1)} %fusion.16), channel_id=1, source_target_pairs={{2,1},{6,5},{10,9},{14,13},{18,17},{22,21},{26,25},{30,29}} | collective-permute-start | bytes 1572872 | tf_op jit(solution)/shard_map/ppermute | solution.py:11
  411.2 21.7 %collective-permute-start.22 = (bf16[512,512]{1,0:T(8,128)(2,1)S(1)}, bf16[512,512]{1,0:T(8,128)(2,1)S(1)}, u32[]{:S(2)}, u32[]{:S(2)}) collective-permute-start(bf16[512,512]{1,0:T(8,128)(2,1)S(1)} %fusion.17), channel_id=1, source_target_pairs={{2,0},{6,4},{10,8},{14,12},{18,16},{22,20},{26,24},{30,28}} | collective-permute-start | bytes 1572872 | tf_op jit(solution)/shard_map/ppermute | solution.py:11
  415.6 36.5 %collective-permute-start.23 = (bf16[512,512]{1,0:T(8,128)(2,1)S(1)}, bf16[512,512]{1,0:T(8,128)(2,1)S(1)}, u32[]{:S(2)}, u32[]{:S(2)}) collective-permute-start(bf16[512,512]{1,0:T(8,128)(2,1)S(1)} %fusion.18), channel_id=1, source_target_pairs={{2,1},{6,5},{10,9},{14,13},{18,17},{22,21},{26,25},{30,29}} | collective-permute-start | bytes 1572872 | tf_op jit(solution)/shard_map/ppermute | solution.py:11
  452.4 2.4 copy-start.1
  (5 other events, 8.5 us)
